TPU v7x, 32 devices: a whole 2x2x4 slice. The times are simulated.
32 devices in a mesh: tok: 8 (over z, x), ch: 4 (over y, core).
Axes of the slice: x: 2, y: 2, z: 4, core: 2. Of those that a mesh axis runs over, the one named last changes fastest.
Arguments:
- tokens: bfloat16 [262144, 1024], P('tok', 'ch'), may hold values from -6 to 6
- w_value: bfloat16 [1024, 1024], P(None, 'ch'), may hold values from -0.1875 to 0.1875
- w_gate: bfloat16 [1024, 1024], P(None, 'ch'), may hold values from -0.1875 to 0.1875
- first_factor: bfloat16 [512, 512], replicated, may hold values from -0.25 to 0.25
- twiddle: float32 [512, 512], P('tok'), may hold values from 0.5 to 1.5
- second_factor: float32 [512, 512], replicated, may hold values from -0.25 to 0.25
- freq_kernel: float32 [512, 1024], P('tok', 'ch'), may hold values from -5 to 5
- row_kernel: float32 [512, 1024], P(None, 'ch'), may hold values from -5 to 5
- inverse_first: float32 [512, 512], replicated, may hold values from -0.25 to 0.25
- inverse_second: float32 [512, 512], replicated, may hold values from -0.25 to 0.25
Outputs:
- mixed: bfloat16 [262144, 1024], P('tok', 'ch')
All inputs are finite; a program needn't handle non-finite values.
Results may differ from a plain program's by a relative error of at most 0.0049.
Values may be sent and summed in bfloat16 or wider, within the bound.
No kernel may reach another device: no remote copies, remote signals or barrier semaphores. Data moves between devices by JAX's collectives and lax.ppermute only.
A program may use at most 192 MiB of HBM per device.

v0:
```python
import functools

import jax
import jax.numpy as jnp
from jax import lax
from jax.experimental import pallas as pl
from jax.experimental.pallas import tpu as pltpu
from jax.sharding import PartitionSpec as P

BLOCK = 512
CHUNK = 8
GROUP = 16
HALF = 128
STEP = 2
WIDE = 4
VMEM = 56 * 2**20

WHOLE = pl.BlockSpec(memory_space=pltpu.SMEM)


def params():
    return pltpu.CompilerParams(vmem_limit_bytes=VMEM, dimension_semantics=("arbitrary",))


def full(array):
    return pl.BlockSpec(array.shape, lambda s: (0,) * array.ndim)


def wide_dot(left, right):
    return jnp.dot(left, right, preferred_element_type=jnp.float32)


def store_parts(parts_ref, matrix_ref):
    rows = matrix_ref.shape[0]
    matrix = matrix_ref[...]
    upper = matrix.astype(jnp.bfloat16)
    parts_ref[:rows] = upper
    parts_ref[rows:] = (matrix - upper.astype(jnp.float32)).astype(jnp.bfloat16)


def split_dot(parts_ref, right):
    both = wide_dot(parts_ref[...], right)
    rows = both.shape[0] // 2
    return both[:rows] + both[rows:]


def first_body(order, parts, halves, at_ref, *refs):
    count = len(order)
    pieces, (value_ref, gate_ref, factor_ref, twiddle_ref) = refs[:count], refs[count : count + 4]
    outs, (scratch_a, scratch_b, weights, columns) = refs[count + 4 : -4], refs[-4:]
    scratch = (scratch_a, scratch_b)
    step = pl.program_id(0)
    channels = value_ref.shape[1]
    rows = twiddle_ref.shape[0]

    @pl.when(step == 0)
    def _():
        for place, side in enumerate(order):
            begin = pl.multiple_of((at_ref[0] ^ side) * channels, channels)
            here = slice(place * channels, (place + 1) * channels)
            weights[here, :channels] = value_ref[pl.ds(begin, channels), :]
            weights[here, channels:] = gate_ref[pl.ds(begin, channels), :]
        padding = jnp.zeros((128 - rows, BLOCK), jnp.float32)
        columns[...] = jnp.concatenate([twiddle_ref[...], padding], axis=0).T

    both = wide_dot(jnp.concatenate([piece[...] for piece in pieces], axis=1), weights[...])
    value, gate = both[:, :channels], both[:, channels:]
    gated = (value * (gate / (1.0 + jnp.exp(-gate)))).astype(jnp.bfloat16)
    lanes = lax.broadcasted_iota(jnp.int32, columns.shape, 1)
    for row in range(STEP):
        at = step * STEP + row
        scale = jnp.sum(jnp.where(lanes == at, columns[...], 0.0), axis=1, keepdims=True)
        section = wide_dot(factor_ref[...], gated[row * BLOCK : (row + 1) * BLOCK]) * scale
        for half in range(2):
            scratch[half][pl.ds(at, BLOCK, stride=rows), :] = section[:, half * HALF : (half + 1) * HALF]

    @pl.when(step == pl.num_programs(0) - 1)
    def _():
        size = BLOCK // parts * rows
        for part in range(parts):
            for half in range(2):
                block = scratch[half][part * size : (part + 1) * size, :].astype(jnp.bfloat16)
                if halves:
                    outs[half][part] = block
                else:
                    outs[0][part, :, half * HALF : (half + 1) * HALF] = block


def first_section(at, pieces, order, begin, rows, w_value, w_gate, factor, twiddle, parts, halves):
    channels = w_value.shape[1]
    depth, patches = w_value.shape[0], rows * BLOCK
    inner = BLOCK // parts
    widths = [HALF, HALF] if halves else [channels]
    outs = [jax.ShapeDtypeStruct((parts, inner * rows, width), jnp.bfloat16) for width in widths]
    return pl.pallas_call(
        functools.partial(first_body, order, parts, halves),
        grid=(rows // STEP,),
        in_specs=[WHOLE]
        + [
            pl.BlockSpec((STEP * BLOCK, piece.shape[1]), lambda s, start=start: (start // STEP + s, 0))
            for piece, start in zip(pieces, [begin] + [0] * len(pieces))
        ]
        + [full(w_value), full(w_gate), full(factor), pl.BlockSpec((rows, BLOCK), lambda s: (begin // rows, 0))],
        out_specs=[full(out) for out in outs],
        out_shape=outs,
        scratch_shapes=[pltpu.VMEM((BLOCK * rows, HALF), jnp.float32)] * 2
        + [pltpu.VMEM((depth, 2 * channels), jnp.bfloat16), pltpu.VMEM((BLOCK, 128), jnp.float32)],
        compiler_params=params(),
        cost_estimate=pl.CostEstimate(
            flops=2 * patches * channels * (2 * depth + BLOCK),
            bytes_accessed=2 * patches * (depth + channels),
            transcendentals=patches * channels,
        ),
        name="project_and_mix_rows",
    )(at, *pieces, w_value, w_gate, factor, twiddle)


def middle_body(chunks, parts, splits, *refs):
    blocks = refs[:chunks]
    second_ref, inverse_ref, freq_ref, row_ref = refs[chunks : chunks + 4]
    outs, (second, inverse, gathered, scratch) = refs[chunks + 4 : -4], refs[-4:]
    local_rows = chunks * CHUNK

    @pl.when(pl.program_id(0) == 0)
    def _():
        store_parts(second, second_ref)
        store_parts(inverse, inverse_ref)

    @pl.loop(0, GROUP // 2)
    def _(pair):
        start = pl.multiple_of(pair * 2 * CHUNK, 2 * CHUNK)
        lane = pl.multiple_of(pair * 2 * HALF, 2 * HALF)
        for part in range(parts):
            for chunk in range(0, chunks, 2):
                one, two = (
                    blocks[more][part, pl.ds(start, 2 * CHUNK), :].astype(jnp.float32) for more in (chunk, chunk + 1)
                )
                row = part * local_rows + chunk * CHUNK
                for side in range(2):
                    here = slice(side * CHUNK, (side + 1) * CHUNK)
                    tile = jnp.concatenate([one[here], two[here]], axis=0).astype(jnp.bfloat16)
                    gathered[row : row + 2 * CHUNK, pl.ds(pl.multiple_of(lane + side * HALF, HALF), HALF)] = tile

    row_gate = jnp.concatenate([row_ref[...]] * WIDE, axis=1)

    @pl.loop(0, GROUP // WIDE)
    def _(turn):
        lane = pl.multiple_of(turn * WIDE * HALF, WIDE * HALF)
        section = split_dot(second, gathered[:, pl.ds(lane, WIDE * HALF)])
        freq = jnp.concatenate([freq_ref[pl.ds(turn * WIDE + side, 1), :] for side in range(WIDE)], axis=1)
        spectrum = (section * freq * row_gate).astype(jnp.bfloat16)
        section = split_dot(inverse, spectrum)
        for side in range(WIDE):
            scratch[pl.ds(turn * WIDE + side, BLOCK, stride=GROUP), :] = section[:, side * HALF : (side + 1) * HALF]

    inner = BLOCK // parts
    for out, (first, rows) in zip(outs, splits):
        for part in range(parts):
            block = scratch[(part * inner + first) * GROUP : (part * inner + first + rows) * GROUP, :]
            out[part] = block.astype(jnp.bfloat16).reshape(rows, GROUP, HALF)


def middle_section(blocks, places, half, second, inverse, freq, row, parts, splits):
    indices = freq.shape[0]
    outs = [jax.ShapeDtypeStruct((parts, rows, indices, HALF), jnp.bfloat16) for _, rows in splits]
    return pl.pallas_call(
        functools.partial(middle_body, len(blocks), parts, splits),
        grid=(indices // GROUP,),
        in_specs=[
            pl.BlockSpec((parts, GROUP * CHUNK, HALF), lambda s, place=place: (0, s, place)) for place in places
        ]
        + [
            full(second),
            full(inverse),
            pl.BlockSpec((GROUP, HALF), lambda s: (s, half)),
            pl.BlockSpec((BLOCK, HALF), lambda s: (0, half)),
        ],
        out_specs=[pl.BlockSpec((parts, rows, GROUP, HALF), lambda s: (0, 0, s, 0)) for _, rows in splits],
        out_shape=outs,
        scratch_shapes=[pltpu.VMEM((2 * BLOCK, BLOCK), jnp.bfloat16)] * 2
        + [pltpu.VMEM((BLOCK, GROUP * HALF), jnp.bfloat16), pltpu.VMEM((BLOCK * GROUP, HALF), jnp.float32)],
        compiler_params=params(),
        cost_estimate=pl.CostEstimate(
            flops=8 * BLOCK * BLOCK * indices * HALF,
            bytes_accessed=4 * BLOCK * indices * HALF,
            transcendentals=0,
        ),
        name="mix_grid_rows",
    )(*blocks, second, inverse, freq, row)


def last_body(block_ref, inverse_ref, *rest):
    out_ref, inverse, gathered = rest[-3:]
    group = block_ref.shape[1]

    @pl.when(pl.program_id(0) == 0)
    def _():
        store_parts(inverse, inverse_ref)

    for row in range(group):
        gathered[:, row * HALF : (row + 1) * HALF] = block_ref[:, row].reshape(BLOCK, HALF)

    @pl.loop(0, group // WIDE)
    def _(turn):
        lane = pl.multiple_of(turn * WIDE * HALF, WIDE * HALF)
        mixed = split_dot(inverse, gathered[:, pl.ds(lane, WIDE * HALF)]).astype(jnp.bfloat16)
        for side in range(WIDE):
            start = pl.multiple_of((turn * WIDE + side) * BLOCK, BLOCK)
            out_ref[pl.ds(start, BLOCK), :] = mixed[:, side * HALF : (side + 1) * HALF]


def last_section(block, inverse, shape, begin, half, before):
    parts, rows, inner, _ = block.shape
    group = min(rows, 8)
    operands = [block, inverse]
    specs = [pl.BlockSpec((parts, group, inner, HALF), lambda s: (0, s, 0, 0)), full(inverse)]
    aliases = {}
    if before is not None:
        aliases = {len(operands): 0}
        operands.append(before)
        specs.append(pl.BlockSpec(memory_space=pl.ANY))
    return pl.pallas_call(
        last_body,
        grid=(rows // group,),
        in_specs=specs,
        out_specs=pl.BlockSpec((group * BLOCK, HALF), lambda s: (begin // group + s, half)),
        out_shape=jax.ShapeDtypeStruct(shape, jnp.bfloat16),
        input_output_aliases=aliases,
        scratch_shapes=[pltpu.VMEM((2 * BLOCK, BLOCK), jnp.bfloat16), pltpu.VMEM((BLOCK, group * HALF), jnp.bfloat16)],
        compiler_params=params(),
        cost_estimate=pl.CostEstimate(
            flops=4 * BLOCK * BLOCK * rows * HALF,
            bytes_accessed=4 * BLOCK * rows * HALF,
            transcendentals=0,
        ),
        name="mix_rows_back",
    )(*operands)


def swap(x, count, bit):
    return lax.ppermute(x, "ch", [(at, at ^ bit) for at in range(count)])


def exchange(block):
    return lax.all_to_all(block, "tok", split_axis=0, concat_axis=0, tiled=True)


def after(x, before):
    return x if before is None else lax.optimization_barrier((x, before))[0]


def shards(
    parts,
    sides,
    tokens,
    w_value,
    w_gate,
    first_factor,
    twiddle,
    second_factor,
    freq_kernel,
    row_kernel,
    inverse_first,
    inverse_second,
):
    tok_rows, channels = tokens.shape
    local_rows = tok_rows // BLOCK
    chunks = local_rows // CHUNK
    at = lax.axis_index("ch").astype(jnp.int32).reshape(1)
    order = [0]
    bits = [sides >> step for step in range(1, sides.bit_length())]
    for bit in bits:
        order = order + [side ^ bit for side in order]

    size = CHUNK * BLOCK
    owns = [tokens[:size]]
    rest = after(tokens, owns[0])
    owns += [rest[begin : begin + size] for begin in range(size, tok_rows, size)]

    blocks = [[], []]
    places = [[], []]
    before = None
    for chunk, own in enumerate(owns):
        pieces = [own]
        for bit in bits:
            if chunk == 0 and bit == bits[-1]:
                pieces[0] = lax.optimization_barrier((own, *owns[1:]))[0]
            pieces = pieces + [swap(piece, sides, bit) for piece in pieces]
        pieces[0] = tokens
        last = chunk == chunks - 1
        outs = first_section(
            at, pieces, order, chunk * CHUNK, CHUNK, w_value, w_gate, first_factor, twiddle, parts, last
        )
        moved = []
        for out in outs:
            before = exchange(after(out, before))
            moved.append(before)
        for half in range(2):
            blocks[half].append(moved[half if last else 0])
            places[half].append(0 if last else half)

    tail = local_rows // 4
    cuts = [(0, local_rows - tail), (local_rows - tail, tail)] if tail % 8 == 0 else [(0, local_rows)]
    sections = []
    for half, splits in enumerate([[(0, local_rows)], cuts]):
        outs = middle_section(
            blocks[half], places[half], half, second_factor, inverse_first, freq_kernel, row_kernel, parts, splits
        )
        for out, (begin, _) in zip(outs, splits):
            before = exchange(after(out, before))
            sections.append((before, begin, half))
    result = None
    for section, begin, half in sections:
        result = last_section(section, inverse_second, (tok_rows, channels), begin, half, result)
    return result


def solution(mesh):
    return jax.shard_map(
        functools.partial(shards, mesh.shape["tok"], mesh.shape["ch"]),
        mesh=mesh,
        in_specs=(
            P("tok", "ch"),
            P(None, "ch"),
            P(None, "ch"),
            P(),
            P("tok", None),
            P(),
            P("tok", "ch"),
            P(None, "ch"),
            P(),
            P(),
        ),
        out_specs=P("tok", "ch"),
        check_vma=False,
    )
```

profile of v0, /device:TPU:0, one launch (start us, length us, event | category | flops | bytes accessed | tf_op | source)
XLA Modules:
  0.0 888.6 jit_solution(12035841989334536532)
XLA Ops:
  0.0 3.0 slice.24
  3.0 3.0 collective-permute-start
  6.0 10.2 %fusion = (bf16[4096,256]{1,0:T(8,128)(2,1)S(1)}, bf16[4096,256]{1,0:T(8,128)(2,1)}, bf16[4096,256]{1,0:T(8,128)(2,1)}, bf16[4096,256]{1,0:T(8,128)(2,1)}, bf16[...) fusion(bf16[32768,256]{1,0:T(8,128)(2,1)} %refs_0_.15), kind=kLoop, calls=%fused_computation | loop fusion | bytes 29360128 | tf_op jit(solution)/shard_map/slice | solution.py:278
  16.3 35.7 %collective-permute-done.refs_1_ = bf16[4096,256]{1,0:T(8,128)(2,1)} collective-permute-done((bf16[4096,256]{1,0:T(8,128)(2,1)}, bf16[4096,256]{1,0:T(8,128)(2,1)}, u32[]{:S(2)}, u32[]{:S(2)}) %collective-permute-start) | collective-permute-done | bytes 2097184 | tf_op jit(solution)/shard_map/ppermute | solution.py:241
  52.0 1.7 collective-permute-start.3
  53.7 2.8 collective-permute-done.2.refs_3_
  56.5 10.5 %project_and_mix_rows.8 = bf16[8,512,256]{2,1,0:T(8,128)(2,1)} custom-call(s32[1]{0:T(128)} %bitcast.at_ref, bf16[32768,256]{1,0:T(8,128)(2,1)} %refs_0_.15, bf16[4096,256]{1,0:T(8,128)(2,1)} %collective-permute-done.refs_1_, bf16[4096,256]{1,0:T(8,128)(2,1)} %collective-permute-done.1.refs_2_, bf16[4096,256]{1,0:T(8,128)(2,1)} %collective-permute-done.2.refs_3_, ...), custom_call_target="tpu_custom_call" | custom-call | flops 5368709120 | bytes 10485760 | tf_op jit(solution)/shard_map/project_and_mix_rows/pallas_call | solution.py:95
  67.0 6.0 all-to-all-start
  73.0 27.3 %collective-permute-done.3.refs_1_ = bf16[4096,256]{1,0:T(8,128)(2,1)} collective-permute-done((bf16[4096,256]{1,0:T(8,128)(2,1)}, bf16[4096,256]{1,0:T(8,128)(2,1)}, u32[]{:S(2)}, u32[]{:S(2)}) %collective-permute-start.3) | collective-permute-done | bytes 2097184 | tf_op jit(solution)/shard_map/ppermute | solution.py:241
  100.3 1.7 collective-permute-start.6
  102.1 2.6 collective-permute-done.5.refs_3_
  106.1 10.6 %project_and_mix_rows.9 = bf16[8,512,256]{2,1,0:T(8,128)(2,1)} custom-call(s32[1]{0:T(128)} %bitcast.at_ref, bf16[32768,256]{1,0:T(8,128)(2,1)} %refs_0_.15, bf16[4096,256]{1,0:T(8,128)(2,1)} %collective-permute-done.3.refs_1_, bf16[4096,256]{1,0:T(8,128)(2,1)} %copy-done.1, bf16[4096,256]{1,0:T(8,128)(2,1)} %copy-done.7, bf16[1024,256]{1,0:T(8,128)(2,1)} %refs_4_.15, ...), custom_call_target="tpu_custom_call" | custom-call | flops 5368709120 | bytes 10485760 | tf_op jit(solution)/shard_map/project_and_mix_rows/pallas_call | solution.py:95
  116.7 5.0 all-to-all-done.refs_0_
  121.7 4.4 all-to-all-start.1
  126.1 22.6 %collective-permute-done.6.refs_1_ = bf16[4096,256]{1,0:T(8,128)(2,1)} collective-permute-done((bf16[4096,256]{1,0:T(8,128)(2,1)}, bf16[4096,256]{1,0:T(8,128)(2,1)}, u32[]{:S(2)}, u32[]{:S(2)}) %collective-permute-start.6) | collective-permute-done | bytes 2097184 | tf_op jit(solution)/shard_map/ppermute | solution.py:241
  148.7 1.7 collective-permute-start.9
  150.4 2.6 collective-permute-done.8.refs_3_
  154.4 10.6 %project_and_mix_rows.10 = bf16[8,512,256]{2,1,0:T(8,128)(2,1)} custom-call(s32[1]{0:T(128)} %bitcast.at_ref, bf16[32768,256]{1,0:T(8,128)(2,1)} %refs_0_.15, bf16[4096,256]{1,0:T(8,128)(2,1)} %collective-permute-done.6.refs_1_, bf16[4096,256]{1,0:T(8,128)(2,1)} %copy-done.2, bf16[4096,256]{1,0:T(8,128)(2,1)} %copy-done.8, bf16[1024,256]{1,0:T(8,128)(2,1)} %refs_4_.15, ...), custom_call_target="tpu_custom_call" | custom-call | flops 5368709120 | bytes 10485760 | tf_op jit(solution)/shard_map/project_and_mix_rows/pallas_call | solution.py:95
  165.0 8.9 all-to-all-done.1.refs_1_
  173.8 4.4 all-to-all-start.2
  178.3 18.8 %collective-permute-done.9.refs_1_ = bf16[4096,256]{1,0:T(8,128)(2,1)} collective-permute-done((bf16[4096,256]{1,0:T(8,128)(2,1)}, bf16[4096,256]{1,0:T(8,128)(2,1)}, u32[]{:S(2)}, u32[]{:S(2)}) %collective-permute-start.9) | collective-permute-done | bytes 2097184 | tf_op jit(solution)/shard_map/ppermute | solution.py:241
  197.0 1.7 collective-permute-start.12
  198.8 2.6 collective-permute-done.11.refs_3_
  201.4 1.4 copy-done.9
  202.8 10.5 %project_and_mix_rows.11 = bf16[8,512,256]{2,1,0:T(8,128)(2,1)} custom-call(s32[1]{0:T(128)} %bitcast.at_ref, bf16[32768,256]{1,0:T(8,128)(2,1)} %refs_0_.15, bf16[4096,256]{1,0:T(8,128)(2,1)} %collective-permute-done.9.refs_1_, bf16[4096,256]{1,0:T(8,128)(2,1)} %copy-done.3, bf16[4096,256]{1,0:T(8,128)(2,1)} %copy-done.9, bf16[1024,256]{1,0:T(8,128)(2,1)} %refs_4_.15, ...), custom_call_target="tpu_custom_call" | custom-call | flops 5368709120 | bytes 10485760 | tf_op jit(solution)/shard_map/project_and_mix_rows/pallas_call | solution.py:95
  213.4 12.7 %all-to-all-done.2.refs_2_ = bf16[8,512,256]{2,1,0:T(8,128)(2,1)} async-done(((bf16[8,512,256]{2,1,0:T(8,128)(2,1)}), bf16[8,512,256]{2,1,0:T(8,128)(2,1)}, u32[]{:S(2)}, u32[]{:S(2)}) %all-to-all-start.2) | async-done | bytes 2097184 | tf_op jit(solution)/shard_map/all_to_all | solution.py:245
  226.0 4.4 all-to-all-start.3
  230.4 15.0 %collective-permute-done.12.refs_1_ = bf16[4096,256]{1,0:T(8,128)(2,1)} collective-permute-done((bf16[4096,256]{1,0:T(8,128)(2,1)}, bf16[4096,256]{1,0:T(8,128)(2,1)}, u32[]{:S(2)}, u32[]{:S(2)}) %collective-permute-start.12) | collective-permute-done | bytes 2097184 | tf_op jit(solution)/shard_map/ppermute | solution.py:241
  245.4 1.7 collective-permute-start.15
  247.2 2.6 collective-permute-done.14.refs_3_
  249.8 1.4 copy-done.10
  251.1 10.7 %project_and_mix_rows.12 = bf16[8,512,256]{2,1,0:T(8,128)(2,1)} custom-call(s32[1]{0:T(128)} %bitcast.at_ref, bf16[32768,256]{1,0:T(8,128)(2,1)} %refs_0_.15, bf16[4096,256]{1,0:T(8,128)(2,1)} %collective-permute-done.12.refs_1_, bf16[4096,256]{1,0:T(8,128)(2,1)} %copy-done.4, bf16[4096,256]{1,0:T(8,128)(2,1)} %copy-done.10, bf16[1024,256]{1,0:T(8,128)(2,1)} %refs_4_.15, ...), custom_call_target="tpu_custom_call" | custom-call | flops 5368709120 | bytes 10485760 | tf_op jit(solution)/shard_map/project_and_mix_rows/pallas_call | solution.py:95
  261.8 16.3 %all-to-all-done.3.refs_3_ = bf16[8,512,256]{2,1,0:T(8,128)(2,1)} async-done(((bf16[8,512,256]{2,1,0:T(8,128)(2,1)}), bf16[8,512,256]{2,1,0:T(8,128)(2,1)}, u32[]{:S(2)}, u32[]{:S(2)}) %all-to-all-start.3) | async-done | bytes 2097184 | tf_op jit(solution)/shard_map/all_to_all | solution.py:245
  278.2 4.5 all-to-all-start.4
  282.8 11.0 %collective-permute-done.15.refs_1_ = bf16[4096,256]{1,0:T(8,128)(2,1)} collective-permute-done((bf16[4096,256]{1,0:T(8,128)(2,1)}, bf16[4096,256]{1,0:T(8,128)(2,1)}, u32[]{:S(2)}, u32[]{:S(2)}) %collective-permute-start.15) | collective-permute-done | bytes 2097184 | tf_op jit(solution)/shard_map/ppermute | solution.py:241
  293.8 1.7 collective-permute-start.18
  295.5 2.6 collective-permute-done.17.refs_3_
  298.1 1.4 copy-done.11
  299.5 10.6 %project_and_mix_rows.13 = bf16[8,512,256]{2,1,0:T(8,128)(2,1)} custom-call(s32[1]{0:T(128)} %bitcast.at_ref, bf16[32768,256]{1,0:T(8,128)(2,1)} %refs_0_.15, bf16[4096,256]{1,0:T(8,128)(2,1)} %collective-permute-done.15.refs_1_, bf16[4096,256]{1,0:T(8,128)(2,1)} %copy-done.5, bf16[4096,256]{1,0:T(8,128)(2,1)} %copy-done.11, bf16[1024,256]{1,0:T(8,128)(2,1)} %refs_4_.15, ...), custom_call_target="tpu_custom_call" | custom-call | flops 5368709120 | bytes 10485760 | tf_op jit(solution)/shard_map/project_and_mix_rows/pallas_call | solution.py:95
  310.1 20.3 %all-to-all-done.4.refs_4_ = bf16[8,512,256]{2,1,0:T(8,128)(2,1)} async-done(((bf16[8,512,256]{2,1,0:T(8,128)(2,1)}), bf16[8,512,256]{2,1,0:T(8,128)(2,1)}, u32[]{:S(2)}, u32[]{:S(2)}) %all-to-all-start.4) | async-done | bytes 2097184 | tf_op jit(solution)/shard_map/all_to_all | solution.py:245
  330.4 4.4 all-to-all-start.5
  334.9 7.3 collective-permute-done.18.refs_1_
  342.1 1.7 collective-permute-start.21
  343.9 2.6 collective-permute-done.20.refs_3_
  346.5 1.4 copy-done.12
  347.9 10.6 %project_and_mix_rows.14 = bf16[8,512,256]{2,1,0:T(8,128)(2,1)} custom-call(s32[1]{0:T(128)} %bitcast.at_ref, bf16[32768,256]{1,0:T(8,128)(2,1)} %refs_0_.15, bf16[4096,256]{1,0:T(8,128)(2,1)} %collective-permute-done.18.refs_1_, bf16[4096,256]{1,0:T(8,128)(2,1)} %copy-done.6, bf16[4096,256]{1,0:T(8,128)(2,1)} %copy-done.12, bf16[1024,256]{1,0:T(8,128)(2,1)} %refs_4_.15, ...), custom_call_target="tpu_custom_call" | custom-call | flops 5368709120 | bytes 10485760 | tf_op jit(solution)/shard_map/project_and_mix_rows/pallas_call | solution.py:95
  358.5 24.0 %all-to-all-done.5.refs_5_ = bf16[8,512,256]{2,1,0:T(8,128)(2,1)} async-done(((bf16[8,512,256]{2,1,0:T(8,128)(2,1)}), bf16[8,512,256]{2,1,0:T(8,128)(2,1)}, u32[]{:S(2)}, u32[]{:S(2)}) %all-to-all-start.5) | async-done | bytes 2097184 | tf_op jit(solution)/shard_map/all_to_all | solution.py:245
  382.5 4.3 all-to-all-start.6
  386.9 3.4 collective-permute-done.21.refs_1_
  391.1 3.6 collective-permute-done.23.refs_3_
  396.0 10.5 %project_and_mix_rows.15 = (bf16[8,512,128]{2,1,0:T(8,128)(2,1)}, bf16[8,512,128]{2,1,0:T(8,128)(2,1)}) custom-call(s32[1]{0:T(128)} %bitcast.at_ref, bf16[32768,256]{1,0:T(8,128)(2,1)} %refs_0_.15, bf16[4096,256]{1,0:T(8,128)(2,1)} %collective-permute-done.21.refs_1_, bf16[4096,256]{1,0:T(8,128)(2,1)} %copy-done.13, bf16[4096,256]{1,0:T(8,128)(2,1)} %copy-done.14, ...), custom_call_target="tpu_custom_call" | custom-call | flops 5368709120 | bytes 10485760 | tf_op jit(solution)/shard_map/project_and_mix_rows/pallas_call | solution.py:95
  406.5 28.1 %all-to-all-done.6.refs_6_ = bf16[8,512,256]{2,1,0:T(8,128)(2,1)} async-done(((bf16[8,512,256]{2,1,0:T(8,128)(2,1)}), bf16[8,512,256]{2,1,0:T(8,128)(2,1)}, u32[]{:S(2)}, u32[]{:S(2)}) %all-to-all-start.6) | async-done | bytes 2097184 | tf_op jit(solution)/shard_map/all_to_all | solution.py:245
  434.7 29.7 %all_to_all.60.refs_7_ = bf16[8,512,128]{2,1,0:T(8,128)(2,1)} all-to-all(bf16[8,512,128]{2,1,0:T(8,128)(2,1)} %get-tuple-element.32), channel_id=1, replica_groups=mesh['tok'=8,'ch'=4] {'tok'}, dimensions={0} | all-to-all | bytes 2097152 | tf_op jit(solution)/shard_map/all_to_all | solution.py:245
  464.4 3.6 all-to-all-start.8
  467.9 30.8 %mix_grid_rows.3 = bf16[8,64,64,128]{3,2,1,0:T(8,128)(2,1)} custom-call(bf16[8,512,256]{2,1,0:T(8,128)(2,1)} %all-to-all-done.refs_0_, bf16[8,512,256]{2,1,0:T(8,128)(2,1)} %all-to-all-done.1.refs_1_, bf16[8,512,256]{2,1,0:T(8,128)(2,1)} %all-to-all-done.2.refs_2_, bf16[8,512,256]{2,1,0:T(8,128)(2,1)} %all-to-all-done.3.refs_3_, ...), custom_call_target="tpu_custom_call" | custom-call | flops 17179869184 | bytes 16777216 | tf_op jit(solution)/shard_map/mix_grid_rows/pallas_call | solution.py:166
  499.8 6.0 all-to-all-start.9
  505.7 30.9 %mix_grid_rows.2 = (bf16[8,48,64,128]{3,2,1,0:T(8,128)(2,1)}, bf16[8,16,64,128]{3,2,1,0:T(8,128)(2,1)}) custom-call(bf16[8,512,256]{2,1,0:T(8,128)(2,1)} %all-to-all-done.refs_0_, bf16[8,512,256]{2,1,0:T(8,128)(2,1)} %all-to-all-done.1.refs_1_, bf16[8,512,256]{2,1,0:T(8,128)(2,1)} %all-to-all-done.2.refs_2_, bf16[8,512,256]{2,1,0:T(8,128)(2,1)} %all-to-all-done.3.refs_3_, ...), custom_call_target="tpu_custom_call" | custom-call | flops 17179869184 | bytes 16777216 | tf_op jit(solution)/shard_map/mix_grid_rows/pallas_call | solution.py:166
  536.6 151.3 %all-to-all-done.9.block_ref = bf16[8,64,64,128]{3,2,1,0:T(8,128)(2,1)} async-done(((bf16[8,64,64,128]{3,2,1,0:T(8,128)(2,1)}), bf16[8,64,64,128]{3,2,1,0:T(8,128)(2,1)}, u32[]{:S(2)}, u32[]{:S(2)}) %all-to-all-start.9) | async-done | bytes 8388640 | tf_op jit(solution)/shard_map/all_to_all | solution.py:245
  687.9 142.0 %all_to_all.61.block_ref = bf16[8,48,64,128]{3,2,1,0:T(8,128)(2,1)} all-to-all(bf16[8,48,64,128]{3,2,1,0:T(8,128)(2,1)} %get-tuple-element.37), channel_id=1, replica_groups=mesh['tok'=8,'ch'=4] {'tok'}, dimensions={0} | all-to-all | bytes 12582912 | tf_op jit(solution)/shard_map/all_to_all | solution.py:245
  829.9 4.0 all-to-all-start.11
  833.9 17.1 %mix_rows_back.3.rest_0_ = bf16[32768,256]{1,0:T(8,128)(2,1)} custom-call(bf16[8,64,64,128]{3,2,1,0:T(8,128)(2,1)} %all-to-all-done.9.block_ref, f32[512,512]{1,0:T(8,128)} %inverse_ref.5), custom_call_target="tpu_custom_call" | custom-call | flops 8589934592 | bytes 16777216 | tf_op jit(solution)/shard_map/mix_rows_back/pallas_call | solution.py:222
  851.0 13.5 %mix_rows_back.4.rest_0_ = bf16[32768,256]{1,0:T(8,128)(2,1)} custom-call(bf16[8,48,64,128]{3,2,1,0:T(8,128)(2,1)} %all_to_all.61.block_ref, f32[512,512]{1,0:T(8,128)} %inverse_ref.5, bf16[32768,256]{1,0:T(8,128)(2,1)} %mix_rows_back.3.rest_0_), custom_call_target="tpu_custom_call", output_to_operand_aliasing={{}: (2, {})} | custom-call | flops 6442450944 | bytes 12582912 | tf_op jit(solution)/shard_map/mix_rows_back/pallas_call | solution.py:222
  864.4 16.6 %all-to-all-done.11.block_ref = bf16[8,16,64,128]{3,2,1,0:T(8,128)(2,1)S(1)} async-done(((bf16[8,16,64,128]{3,2,1,0:T(8,128)(2,1)}), bf16[8,16,64,128]{3,2,1,0:T(8,128)(2,1)S(1)}, u32[]{:S(2)}, u32[]{:S(2)}) %all-to-all-start.11) | async-done | bytes 2097184 | tf_op jit(solution)/shard_map/all_to_all | solution.py:245
  882.3 6.2 mix_rows_back.5
  (53 shorter events, 7.8 us)
Async XLA Ops:
  3.0 48.9 %collective-permute-start = (bf16[4096,256]{1,0:T(8,128)(2,1)}, bf16[4096,256]{1,0:T(8,128)(2,1)}, u32[]{:S(2)}, u32[]{:S(2)}) collective-permute-start(bf16[4096,256]{1,0:T(8,128)(2,1)} %slice.24), channel_id=1, source_target_pairs={{0,2},{1,3},{2,0},{3,1},{4,6},{5,7},{6,4},{7,5},{8,10},{9,11},{10,... | collective-permute-start | bytes 6291464 | tf_op jit(solution)/shard_map/ppermute | solution.py:241
  16.2 37.5 %collective-permute-start.1 = (bf16[4096,256]{1,0:T(8,128)(2,1)}, bf16[4096,256]{1,0:T(8,128)(2,1)}, u32[]{:S(2)}, u32[]{:S(2)}) collective-permute-start(bf16[4096,256]{1,0:T(8,128)(2,1)} %slice.24), channel_id=1, source_target_pairs={{0,1},{1,0},{2,3},{3,2},{4,5},{5,4},{6,7},{7,6},{8,9},{9,8},{10,11... | collective-permute-start | bytes 6291464 | tf_op jit(solution)/shard_map/ppermute | solution.py:241
  52.0 4.5 collective-permute-start.2
  52.0 48.4 %collective-permute-start.3 = (bf16[4096,256]{1,0:T(8,128)(2,1)}, bf16[4096,256]{1,0:T(8,128)(2,1)}, u32[]{:S(2)}, u32[]{:S(2)}) collective-permute-start(bf16[4096,256]{1,0:T(8,128)(2,1)} %get-tuple-element.45), channel_id=1, source_target_pairs={{0,2},{1,3},{2,0},{3,1},{4,6},{5,7},{6,4},{7,5},{8,10},{9,11},{10,... | collective-permute-start | bytes 6291464 | tf_op jit(solution)/shard_map/ppermute | solution.py:241
  67.0 54.7 %all-to-all-start = ((bf16[8,512,256]{2,1,0:T(8,128)(2,1)}), bf16[8,512,256]{2,1,0:T(8,128)(2,1)}, u32[]{:S(2)}, u32[]{:S(2)}) async-start(bf16[8,512,256]{2,1,0:T(8,128)(2,1)} %project_and_mix_rows.8), calls=%async_computation | async-start | bytes 4194304 | tf_op jit(solution)/shard_map/all_to_all | solution.py:245
  73.0 29.0 %collective-permute-start.4 = (bf16[4096,256]{1,0:T(8,128)(2,1)}, bf16[4096,256]{1,0:T(8,128)(2,1)S(1)}, u32[]{:S(2)}, u32[]{:S(2)}) collective-permute-start(bf16[4096,256]{1,0:T(8,128)(2,1)} %get-tuple-element.45), channel_id=1, source_target_pairs={{0,1},{1,0},{2,3},{3,2},{4,5},{5,4},{6,7},{7,6},{8,9},{9,8},{10,11... | collective-permute-start | bytes 6291464 | tf_op jit(solution)/shard_map/ppermute | solution.py:241
  100.3 4.4 collective-permute-start.5
  100.3 48.4 %collective-permute-start.6 = (bf16[4096,256]{1,0:T(8,128)(2,1)}, bf16[4096,256]{1,0:T(8,128)(2,1)}, u32[]{:S(2)}, u32[]{:S(2)}) collective-permute-start(bf16[4096,256]{1,0:T(8,128)(2,1)} %get-tuple-element.44), channel_id=1, source_target_pairs={{0,2},{1,3},{2,0},{3,1},{4,6},{5,7},{6,4},{7,5},{8,10},{9,11},{10,... | collective-permute-start | bytes 6291464 | tf_op jit(solution)/shard_map/ppermute | solution.py:241
  102.1 2.6 copy-start.1
  104.7 1.4 copy-start.7
  121.7 52.2 %all-to-all-start.1 = ((bf16[8,512,256]{2,1,0:T(8,128)(2,1)}), bf16[8,512,256]{2,1,0:T(8,128)(2,1)}, u32[]{:S(2)}, u32[]{:S(2)}) async-start(bf16[8,512,256]{2,1,0:T(8,128)(2,1)} %project_and_mix_rows.9), calls=%async_computation.1 | async-start | bytes 4194304 | tf_op jit(solution)/shard_map/all_to_all | solution.py:245
  126.0 24.4 %collective-permute-start.7 = (bf16[4096,256]{1,0:T(8,128)(2,1)}, bf16[4096,256]{1,0:T(8,128)(2,1)S(1)}, u32[]{:S(2)}, u32[]{:S(2)}) collective-permute-start(bf16[4096,256]{1,0:T(8,128)(2,1)} %get-tuple-element.44), channel_id=1, source_target_pairs={{0,1},{1,0},{2,3},{3,2},{4,5},{5,4},{6,7},{7,6},{8,9},{9,8},{10,11... | collective-permute-start | bytes 6291464 | tf_op jit(solution)/shard_map/ppermute | solution.py:241
  148.7 4.4 collective-permute-start.8
  148.7 48.4 %collective-permute-start.9 = (bf16[4096,256]{1,0:T(8,128)(2,1)}, bf16[4096,256]{1,0:T(8,128)(2,1)}, u32[]{:S(2)}, u32[]{:S(2)}) collective-permute-start(bf16[4096,256]{1,0:T(8,128)(2,1)} %get-tuple-element.43), channel_id=1, source_target_pairs={{0,2},{1,3},{2,0},{3,1},{4,6},{5,7},{6,4},{7,5},{8,10},{9,11},{10,... | collective-permute-start | bytes 6291464 | tf_op jit(solution)/shard_map/ppermute | solution.py:241
  150.4 2.6 copy-start.2
  153.1 1.3 copy-start.8
  173.8 52.2 %all-to-all-start.2 = ((bf16[8,512,256]{2,1,0:T(8,128)(2,1)}), bf16[8,512,256]{2,1,0:T(8,128)(2,1)}, u32[]{:S(2)}, u32[]{:S(2)}) async-start(bf16[8,512,256]{2,1,0:T(8,128)(2,1)} %project_and_mix_rows.10), calls=%async_computation.2 | async-start | bytes 4194304 | tf_op jit(solution)/shard_map/all_to_all | solution.py:245
  178.2 20.6 %collective-permute-start.10 = (bf16[4096,256]{1,0:T(8,128)(2,1)}, bf16[4096,256]{1,0:T(8,128)(2,1)S(1)}, u32[]{:S(2)}, u32[]{:S(2)}) collective-permute-start(bf16[4096,256]{1,0:T(8,128)(2,1)} %get-tuple-element.43), channel_id=1, source_target_pairs={{0,1},{1,0},{2,3},{3,2},{4,5},{5,4},{6,7},{7,6},{8,9},{9,8},{10,11... | collective-permute-start | bytes 6291464 | tf_op jit(solution)/shard_map/ppermute | solution.py:241
  197.0 4.4 collective-permute-start.11
  197.0 48.4 %collective-permute-start.12 = (bf16[4096,256]{1,0:T(8,128)(2,1)}, bf16[4096,256]{1,0:T(8,128)(2,1)}, u32[]{:S(2)}, u32[]{:S(2)}) collective-permute-start(bf16[4096,256]{1,0:T(8,128)(2,1)} %get-tuple-element.42), channel_id=1, source_target_pairs={{0,2},{1,3},{2,0},{3,1},{4,6},{5,7},{6,4},{7,5},{8,10},{9,11},{10,... | collective-permute-start | bytes 6291464 | tf_op jit(solution)/shard_map/ppermute | solution.py:241
  198.8 2.6 copy-start.3
  201.4 1.4 copy-start.9
  226.0 52.2 %all-to-all-start.3 = ((bf16[8,512,256]{2,1,0:T(8,128)(2,1)}), bf16[8,512,256]{2,1,0:T(8,128)(2,1)}, u32[]{:S(2)}, u32[]{:S(2)}) async-start(bf16[8,512,256]{2,1,0:T(8,128)(2,1)} %project_and_mix_rows.11), calls=%async_computation.3 | async-start | bytes 4194304 | tf_op jit(solution)/shard_map/all_to_all | solution.py:245
  230.4 16.8 %collective-permute-start.13 = (bf16[4096,256]{1,0:T(8,128)(2,1)}, bf16[4096,256]{1,0:T(8,128)(2,1)S(1)}, u32[]{:S(2)}, u32[]{:S(2)}) collective-permute-start(bf16[4096,256]{1,0:T(8,128)(2,1)} %get-tuple-element.42), channel_id=1, source_target_pairs={{0,1},{1,0},{2,3},{3,2},{4,5},{5,4},{6,7},{7,6},{8,9},{9,8},{10,11... | collective-permute-start | bytes 6291464 | tf_op jit(solution)/shard_map/ppermute | solution.py:241
  245.4 4.4 collective-permute-start.14
  245.4 48.4 %collective-permute-start.15 = (bf16[4096,256]{1,0:T(8,128)(2,1)}, bf16[4096,256]{1,0:T(8,128)(2,1)}, u32[]{:S(2)}, u32[]{:S(2)}) collective-permute-start(bf16[4096,256]{1,0:T(8,128)(2,1)} %get-tuple-element.41), channel_id=1, source_target_pairs={{0,2},{1,3},{2,0},{3,1},{4,6},{5,7},{6,4},{7,5},{8,10},{9,11},{10,... | collective-permute-start | bytes 6291464 | tf_op jit(solution)/shard_map/ppermute | solution.py:241
  247.2 2.6 copy-start.4
  249.8 1.4 copy-start.10
  278.2 52.3 %all-to-all-start.4 = ((bf16[8,512,256]{2,1,0:T(8,128)(2,1)}), bf16[8,512,256]{2,1,0:T(8,128)(2,1)}, u32[]{:S(2)}, u32[]{:S(2)}) async-start(bf16[8,512,256]{2,1,0:T(8,128)(2,1)} %project_and_mix_rows.12), calls=%async_computation.4 | async-start | bytes 4194304 | tf_op jit(solution)/shard_map/all_to_all | solution.py:245
  282.7 12.8 %collective-permute-start.16 = (bf16[4096,256]{1,0:T(8,128)(2,1)}, bf16[4096,256]{1,0:T(8,128)(2,1)S(1)}, u32[]{:S(2)}, u32[]{:S(2)}) collective-permute-start(bf16[4096,256]{1,0:T(8,128)(2,1)} %get-tuple-element.41), channel_id=1, source_target_pairs={{0,1},{1,0},{2,3},{3,2},{4,5},{5,4},{6,7},{7,6},{8,9},{9,8},{10,11... | collective-permute-start | bytes 6291464 | tf_op jit(solution)/shard_map/ppermute | solution.py:241
  293.8 4.4 collective-permute-start.17
  293.8 48.4 %collective-permute-start.18 = (bf16[4096,256]{1,0:T(8,128)(2,1)}, bf16[4096,256]{1,0:T(8,128)(2,1)}, u32[]{:S(2)}, u32[]{:S(2)}) collective-permute-start(bf16[4096,256]{1,0:T(8,128)(2,1)} %get-tuple-element.40), channel_id=1, source_target_pairs={{0,2},{1,3},{2,0},{3,1},{4,6},{5,7},{6,4},{7,5},{8,10},{9,11},{10,... | collective-permute-start | bytes 6291464 | tf_op jit(solution)/shard_map/ppermute | solution.py:241
  295.5 2.6 copy-start.5
  298.1 1.4 copy-start.11
  330.4 52.1 %all-to-all-start.5 = ((bf16[8,512,256]{2,1,0:T(8,128)(2,1)}), bf16[8,512,256]{2,1,0:T(8,128)(2,1)}, u32[]{:S(2)}, u32[]{:S(2)}) async-start(bf16[8,512,256]{2,1,0:T(8,128)(2,1)} %project_and_mix_rows.13), calls=%async_computation.5 | async-start | bytes 4194304 | tf_op jit(solution)/shard_map/all_to_all | solution.py:245
  334.8 9.1 %collective-permute-start.19 = (bf16[4096,256]{1,0:T(8,128)(2,1)}, bf16[4096,256]{1,0:T(8,128)(2,1)S(1)}, u32[]{:S(2)}, u32[]{:S(2)}) collective-permute-start(bf16[4096,256]{1,0:T(8,128)(2,1)} %get-tuple-element.40), channel_id=1, source_target_pairs={{0,1},{1,0},{2,3},{3,2},{4,5},{5,4},{6,7},{7,6},{8,9},{9,8},{10,11... | collective-permute-start | bytes 6291464 | tf_op jit(solution)/shard_map/ppermute | solution.py:241
  342.1 4.4 collective-permute-start.20
  342.1 48.1 %collective-permute-start.21 = (bf16[4096,256]{1,0:T(8,128)(2,1)S(1)}, bf16[4096,256]{1,0:T(8,128)(2,1)}, u32[]{:S(2)}, u32[]{:S(2)}) collective-permute-start(bf16[4096,256]{1,0:T(8,128)(2,1)S(1)} %get-tuple-element.39), channel_id=1, source_target_pairs={{0,2},{1,3},{2,0},{3,1},{4,6},{5,7},{6,4},{7,5},{8,10},{9,11},{10,... | collective-permute-start | bytes 6291464 | tf_op jit(solution)/shard_map/ppermute | solution.py:241
  343.9 2.6 copy-start.6
  346.5 1.4 copy-start.12
  382.5 52.2 %all-to-all-start.6 = ((bf16[8,512,256]{2,1,0:T(8,128)(2,1)}), bf16[8,512,256]{2,1,0:T(8,128)(2,1)}, u32[]{:S(2)}, u32[]{:S(2)}) async-start(bf16[8,512,256]{2,1,0:T(8,128)(2,1)} %project_and_mix_rows.14), calls=%async_computation.6 | async-start | bytes 4194304 | tf_op jit(solution)/shard_map/all_to_all | solution.py:245
  386.8 4.2 collective-permute-start.22
  390.3 4.4 collective-permute-start.23
  391.1 3.6 copy-start.13
  394.6 1.4 copy-start.14
  464.4 34.4 %all-to-all-start.8 = ((bf16[8,512,128]{2,1,0:T(8,128)(2,1)}), bf16[8,512,128]{2,1,0:T(8,128)(2,1)S(1)}, u32[]{:S(2)}, u32[]{:S(2)}) async-start(bf16[8,512,128]{2,1,0:T(8,128)(2,1)} %get-tuple-element.33), calls=%async_computation.8 | async-start | bytes 2097152 | tf_op jit(solution)/shard_map/all_to_all | solution.py:245
  498.8 1.0 copy-start.15
  499.8 188.1 %all-to-all-start.9 = ((bf16[8,64,64,128]{3,2,1,0:T(8,128)(2,1)}), bf16[8,64,64,128]{3,2,1,0:T(8,128)(2,1)}, u32[]{:S(2)}, u32[]{:S(2)}) async-start(bf16[8,64,64,128]{3,2,1,0:T(8,128)(2,1)} %mix_grid_rows.3), calls=%async_computation.9 | async-start | bytes 16777216 | tf_op jit(solution)/shard_map/all_to_all | solution.py:245
  829.9 51.1 %all-to-all-start.11 = ((bf16[8,16,64,128]{3,2,1,0:T(8,128)(2,1)}), bf16[8,16,64,128]{3,2,1,0:T(8,128)(2,1)S(1)}, u32[]{:S(2)}, u32[]{:S(2)}) async-start(bf16[8,16,64,128]{3,2,1,0:T(8,128)(2,1)} %get-tuple-element.38), calls=%async_computation.11 | async-start | bytes 4194304 | tf_op jit(solution)/shard_map/all_to_all | solution.py:245
  881.0 1.4 copy-start
where the time goes:
time: 890 us; the launch traced here: 889 us
  waiting for transfers between devices  447 us (50%)
  Pallas kernels  183 us (21%)
  blocking collectives  172 us (19%)
  starting transfers between devices  61.6 us (7%)
  local copies, waits for them, and re-layouts  25.2 us (3%)
    all_to_all x10, waiting for transfers between devices, exchange(): return lax.all_to_all(block, 'tok', split_axis=0, concat_axis=0, tiled=True)  283 us
    all_to_all x2, blocking collectives, exchange(): return lax.all_to_all(block, 'tok', split_axis=0, concat_axis=0, tiled=True)  172 us
    ppermute x24, waiting for transfers between devices, swap(): return lax.ppermute(x, 'ch', [(at, at ^ bit) for at in range(count)])  164 us
    pallas_call x8, Pallas kernels, first_section(): pl.pallas_call(functools.partial(first_body, order, parts, halves), grid=...  84.7 us
    pallas_call x2, Pallas kernels, middle_section(): pl.pallas_call(functools.partial(middle_body, len(blocks), parts, splits)...  61.7 us
    all_to_all x10, starting transfers between devices, exchange(): return lax.all_to_all(block, 'tok', split_axis=0, concat_axis=0, tiled=True)  45.9 us
    pallas_call x3, Pallas kernels, last_section(): pl.pallas_call(last_body, grid=(rows // group,), in_specs=specs, out_spec...  36.8 us
  transfers between devices with their start and end apart: 34, of which 26 were waited for; matrix products, arithmetic and copies ran while one was open for 1% of the time, Pallas kernels for 20%

commit v1 on v0

--- a/solution.py
+++ b/solution.py
@@ -143,7 +143,7 @@
 
     row_gate = jnp.concatenate([row_ref[...]] * WIDE, axis=1)
 
-    @pl.loop(0, GROUP // WIDE)
+    @pl.loop(0, GROUP // WIDE, unroll=True)
     def _(turn):
         lane = pl.multiple_of(turn * WIDE * HALF, WIDE * HALF)
         section = split_dot(second, gathered[:, pl.ds(lane, WIDE * HALF)])
@@ -200,7 +200,7 @@
     for row in range(group):
         gathered[:, row * HALF : (row + 1) * HALF] = block_ref[:, row].reshape(BLOCK, HALF)
 
-    @pl.loop(0, group // WIDE)
+    @pl.loop(0, group // WIDE, unroll=True)
     def _(turn):
         lane = pl.multiple_of(turn * WIDE * HALF, WIDE * HALF)
         mixed = split_dot(inverse, gathered[:, pl.ds(lane, WIDE * HALF)]).astype(jnp.bfloat16)
@@ -299,19 +299,25 @@
             blocks[half].append(moved[half if last else 0])
             places[half].append(0 if last else half)
 
-    tail = local_rows // 4
+    tail = local_rows // 8
     cuts = [(0, local_rows - tail), (local_rows - tail, tail)] if tail % 8 == 0 else [(0, local_rows)]
     sections = []
     for half, splits in enumerate([[(0, local_rows)], cuts]):
         outs = middle_section(
             blocks[half], places[half], half, second_factor, inverse_first, freq_kernel, row_kernel, parts, splits
         )
-        for out, (begin, _) in zip(outs, splits):
-            before = exchange(after(out, before))
-            sections.append((before, begin, half))
+        sections += [(out, begin, half) for out, (begin, _) in zip(outs, splits)]
     result = None
-    for section, begin, half in sections:
-        result = last_section(section, inverse_second, (tok_rows, channels), begin, half, result)
+    moved = []
+    for turn, (section, begin, half) in enumerate(sections):
+        if turn >= 2:
+            out, start, side = moved[turn - 2]
+            result = last_section(out, inverse_second, (tok_rows, channels), start, side, result)
+            section = after(section, result)
+        before = exchange(after(section, before))
+        moved.append((before, begin, half))
+    for out, start, side in moved[max(len(sections) - 2, 0) :]:
+        result = last_section(out, inverse_second, (tok_rows, channels), start, side, result)
     return result
 
 

time: 890 us -> 886 us (level)
  waiting for transfers between devices: 447 us -> 591 us
  blocking collectives: 172 us -> 29.7 us
  Pallas kernels: 183 us -> 172 us
    all_to_all x10 -> x11, waiting for transfers between devices: 283 us -> 427 us  [exchange(): return lax.all_to_all(block, 'tok', split_axis=0, concat_axis=0, tiled=True)]
    all_to_all x2 -> x1, blocking collectives: 172 us -> 29.7 us  [exchange(): return lax.all_to_all(block, 'tok', split_axis=0, concat_axis=0, tiled=True)]
    all_to_all x10 -> x11, starting transfers between devices: 45.9 us -> 50.4 us  [exchange(): return lax.all_to_all(block, 'tok', split_axis=0, concat_axis=0, tiled=True)]
  transfers between devices with their start and end apart: 34 -> 35, of which waited for: 26 -> 27; matrix products, arithmetic and copies ran while one was open for 1% -> 1% of each run, Pallas kernels for 20% -> 19%
where the time goes in v1:
time: 886 us; the launch traced here: 884 us
  waiting for transfers between devices  591 us (67%)
  Pallas kernels  172 us (19%)
  starting transfers between devices  66.1 us (7%)
  blocking collectives  29.7 us (3%)
  local copies, waits for them, and re-layouts  24.8 us (3%)
    all_to_all x11, waiting for transfers between devices, exchange(): return lax.all_to_all(block, 'tok', split_axis=0, concat_axis=0, tiled=True)  427 us
    ppermute x24, waiting for transfers between devices, swap(): return lax.ppermute(x, 'ch', [(at, at ^ bit) for at in range(count)])  164 us
    pallas_call x8, Pallas kernels, first_section(): pl.pallas_call(functools.partial(first_body, order, parts, halves), grid=...  84.6 us
    pallas_call x2, Pallas kernels, middle_section(): pl.pallas_call(functools.partial(middle_body, len(blocks), parts, splits)...  56.5 us
    all_to_all x11, starting transfers between devices, exchange(): return lax.all_to_all(block, 'tok', split_axis=0, concat_axis=0, tiled=True)  50.4 us
    pallas_call x3, Pallas kernels, last_section(): pl.pallas_call(last_body, grid=(rows // group,), in_specs=specs, out_spec...  31.3 us
    all_to_all x1, blocking collectives, exchange(): return lax.all_to_all(block, 'tok', split_axis=0, concat_axis=0, tiled=True)  29.7 us
  transfers between devices with their start and end apart: 35, of which 27 were waited for; matrix products, arithmetic and copies ran while one was open for 1% of the time, Pallas kernels for 19%

profile of v1, /device:TPU:0, one launch (start us, length us, event | category | flops | bytes accessed | tf_op | source)
XLA Modules:
  0.0 884.3 jit_solution(8909212863447686575)
XLA Ops:
  0.0 3.0 slice.24
  3.0 3.0 collective-permute-start
  6.0 10.2 %fusion = (bf16[4096,256]{1,0:T(8,128)(2,1)S(1)}, bf16[4096,256]{1,0:T(8,128)(2,1)}, bf16[4096,256]{1,0:T(8,128)(2,1)}, bf16[4096,256]{1,0:T(8,128)(2,1)}, bf16[...) fusion(bf16[32768,256]{1,0:T(8,128)(2,1)} %refs_0_.15), kind=kLoop, calls=%fused_computation | loop fusion | bytes 29360128 | tf_op jit(solution)/shard_map/slice | solution.py:278
  16.3 35.7 %collective-permute-done.refs_1_ = bf16[4096,256]{1,0:T(8,128)(2,1)} collective-permute-done((bf16[4096,256]{1,0:T(8,128)(2,1)}, bf16[4096,256]{1,0:T(8,128)(2,1)}, u32[]{:S(2)}, u32[]{:S(2)}) %collective-permute-start) | collective-permute-done | bytes 2097184 | tf_op jit(solution)/shard_map/ppermute | solution.py:241
  52.0 1.7 collective-permute-start.3
  53.7 2.8 collective-permute-done.2.refs_3_
  56.5 10.5 %project_and_mix_rows.8 = bf16[8,512,256]{2,1,0:T(8,128)(2,1)} custom-call(s32[1]{0:T(128)} %bitcast.at_ref, bf16[32768,256]{1,0:T(8,128)(2,1)} %refs_0_.15, bf16[4096,256]{1,0:T(8,128)(2,1)} %collective-permute-done.refs_1_, bf16[4096,256]{1,0:T(8,128)(2,1)} %collective-permute-done.1.refs_2_, bf16[4096,256]{1,0:T(8,128)(2,1)} %collective-permute-done.2.refs_3_, ...), custom_call_target="tpu_custom_call" | custom-call | flops 5368709120 | bytes 10485760 | tf_op jit(solution)/shard_map/project_and_mix_rows/pallas_call | solution.py:95
  67.0 6.0 all-to-all-start
  73.0 27.3 %collective-permute-done.3.refs_1_ = bf16[4096,256]{1,0:T(8,128)(2,1)} collective-permute-done((bf16[4096,256]{1,0:T(8,128)(2,1)}, bf16[4096,256]{1,0:T(8,128)(2,1)}, u32[]{:S(2)}, u32[]{:S(2)}) %collective-permute-start.3) | collective-permute-done | bytes 2097184 | tf_op jit(solution)/shard_map/ppermute | solution.py:241
  100.3 1.7 collective-permute-start.6
  102.1 2.6 collective-permute-done.5.refs_3_
  106.0 10.6 %project_and_mix_rows.9 = bf16[8,512,256]{2,1,0:T(8,128)(2,1)} custom-call(s32[1]{0:T(128)} %bitcast.at_ref, bf16[32768,256]{1,0:T(8,128)(2,1)} %refs_0_.15, bf16[4096,256]{1,0:T(8,128)(2,1)} %collective-permute-done.3.refs_1_, bf16[4096,256]{1,0:T(8,128)(2,1)} %copy-done.1, bf16[4096,256]{1,0:T(8,128)(2,1)} %copy-done.7, bf16[1024,256]{1,0:T(8,128)(2,1)} %refs_4_.15, ...), custom_call_target="tpu_custom_call" | custom-call | flops 5368709120 | bytes 10485760 | tf_op jit(solution)/shard_map/project_and_mix_rows/pallas_call | solution.py:95
  116.6 5.1 all-to-all-done.refs_0_
  121.7 4.4 all-to-all-start.1
  126.1 22.6 %collective-permute-done.6.refs_1_ = bf16[4096,256]{1,0:T(8,128)(2,1)} collective-permute-done((bf16[4096,256]{1,0:T(8,128)(2,1)}, bf16[4096,256]{1,0:T(8,128)(2,1)}, u32[]{:S(2)}, u32[]{:S(2)}) %collective-permute-start.6) | collective-permute-done | bytes 2097184 | tf_op jit(solution)/shard_map/ppermute | solution.py:241
  148.7 1.7 collective-permute-start.9
  150.4 2.6 collective-permute-done.8.refs_3_
  154.4 10.6 %project_and_mix_rows.10 = bf16[8,512,256]{2,1,0:T(8,128)(2,1)} custom-call(s32[1]{0:T(128)} %bitcast.at_ref, bf16[32768,256]{1,0:T(8,128)(2,1)} %refs_0_.15, bf16[4096,256]{1,0:T(8,128)(2,1)} %collective-permute-done.6.refs_1_, bf16[4096,256]{1,0:T(8,128)(2,1)} %copy-done.2, bf16[4096,256]{1,0:T(8,128)(2,1)} %copy-done.8, bf16[1024,256]{1,0:T(8,128)(2,1)} %refs_4_.15, ...), custom_call_target="tpu_custom_call" | custom-call | flops 5368709120 | bytes 10485760 | tf_op jit(solution)/shard_map/project_and_mix_rows/pallas_call | solution.py:95
  165.0 8.9 %all-to-all-done.1.refs_1_ = bf16[8,512,256]{2,1,0:T(8,128)(2,1)} async-done(((bf16[8,512,256]{2,1,0:T(8,128)(2,1)}), bf16[8,512,256]{2,1,0:T(8,128)(2,1)}, u32[]{:S(2)}, u32[]{:S(2)}) %all-to-all-start.1) | async-done | bytes 2097184 | tf_op jit(solution)/shard_map/all_to_all | solution.py:245
  173.8 4.3 all-to-all-start.2
  178.3 18.8 %collective-permute-done.9.refs_1_ = bf16[4096,256]{1,0:T(8,128)(2,1)} collective-permute-done((bf16[4096,256]{1,0:T(8,128)(2,1)}, bf16[4096,256]{1,0:T(8,128)(2,1)}, u32[]{:S(2)}, u32[]{:S(2)}) %collective-permute-start.9) | collective-permute-done | bytes 2097184 | tf_op jit(solution)/shard_map/ppermute | solution.py:241
  197.0 1.7 collective-permute-start.12
  198.8 2.6 collective-permute-done.11.refs_3_
  201.4 1.4 copy-done.9
  202.8 10.6 %project_and_mix_rows.11 = bf16[8,512,256]{2,1,0:T(8,128)(2,1)} custom-call(s32[1]{0:T(128)} %bitcast.at_ref, bf16[32768,256]{1,0:T(8,128)(2,1)} %refs_0_.15, bf16[4096,256]{1,0:T(8,128)(2,1)} %collective-permute-done.9.refs_1_, bf16[4096,256]{1,0:T(8,128)(2,1)} %copy-done.3, bf16[4096,256]{1,0:T(8,128)(2,1)} %copy-done.9, bf16[1024,256]{1,0:T(8,128)(2,1)} %refs_4_.15, ...), custom_call_target="tpu_custom_call" | custom-call | flops 5368709120 | bytes 10485760 | tf_op jit(solution)/shard_map/project_and_mix_rows/pallas_call | solution.py:95
  213.3 12.6 %all-to-all-done.2.refs_2_ = bf16[8,512,256]{2,1,0:T(8,128)(2,1)} async-done(((bf16[8,512,256]{2,1,0:T(8,128)(2,1)}), bf16[8,512,256]{2,1,0:T(8,128)(2,1)}, u32[]{:S(2)}, u32[]{:S(2)}) %all-to-all-start.2) | async-done | bytes 2097184 | tf_op jit(solution)/shard_map/all_to_all | solution.py:245
  226.0 4.4 all-to-all-start.3
  230.4 15.0 %collective-permute-done.12.refs_1_ = bf16[4096,256]{1,0:T(8,128)(2,1)} collective-permute-done((bf16[4096,256]{1,0:T(8,128)(2,1)}, bf16[4096,256]{1,0:T(8,128)(2,1)}, u32[]{:S(2)}, u32[]{:S(2)}) %collective-permute-start.12) | collective-permute-done | bytes 2097184 | tf_op jit(solution)/shard_map/ppermute | solution.py:241
  245.4 1.7 collective-permute-start.15
  247.2 2.6 collective-permute-done.14.refs_3_
  251.1 10.7 %project_and_mix_rows.12 = bf16[8,512,256]{2,1,0:T(8,128)(2,1)} custom-call(s32[1]{0:T(128)} %bitcast.at_ref, bf16[32768,256]{1,0:T(8,128)(2,1)} %refs_0_.15, bf16[4096,256]{1,0:T(8,128)(2,1)} %collective-permute-done.12.refs_1_, bf16[4096,256]{1,0:T(8,128)(2,1)} %copy-done.4, bf16[4096,256]{1,0:T(8,128)(2,1)} %copy-done.10, bf16[1024,256]{1,0:T(8,128)(2,1)} %refs_4_.15, ...), custom_call_target="tpu_custom_call" | custom-call | flops 5368709120 | bytes 10485760 | tf_op jit(solution)/shard_map/project_and_mix_rows/pallas_call | solution.py:95
  261.8 16.4 %all-to-all-done.3.refs_3_ = bf16[8,512,256]{2,1,0:T(8,128)(2,1)} async-done(((bf16[8,512,256]{2,1,0:T(8,128)(2,1)}), bf16[8,512,256]{2,1,0:T(8,128)(2,1)}, u32[]{:S(2)}, u32[]{:S(2)}) %all-to-all-start.3) | async-done | bytes 2097184 | tf_op jit(solution)/shard_map/all_to_all | solution.py:245
  278.2 4.6 all-to-all-start.4
  282.8 11.0 %collective-permute-done.15.refs_1_ = bf16[4096,256]{1,0:T(8,128)(2,1)} collective-permute-done((bf16[4096,256]{1,0:T(8,128)(2,1)}, bf16[4096,256]{1,0:T(8,128)(2,1)}, u32[]{:S(2)}, u32[]{:S(2)}) %collective-permute-start.15) | collective-permute-done | bytes 2097184 | tf_op jit(solution)/shard_map/ppermute | solution.py:241
  293.8 1.7 collective-permute-start.18
  295.5 2.6 collective-permute-done.17.refs_3_
  298.1 1.4 copy-done.11
  299.5 10.6 %project_and_mix_rows.13 = bf16[8,512,256]{2,1,0:T(8,128)(2,1)} custom-call(s32[1]{0:T(128)} %bitcast.at_ref, bf16[32768,256]{1,0:T(8,128)(2,1)} %refs_0_.15, bf16[4096,256]{1,0:T(8,128)(2,1)} %collective-permute-done.15.refs_1_, bf16[4096,256]{1,0:T(8,128)(2,1)} %copy-done.5, bf16[4096,256]{1,0:T(8,128)(2,1)} %copy-done.11, bf16[1024,256]{1,0:T(8,128)(2,1)} %refs_4_.15, ...), custom_call_target="tpu_custom_call" | custom-call | flops 5368709120 | bytes 10485760 | tf_op jit(solution)/shard_map/project_and_mix_rows/pallas_call | solution.py:95
  310.1 20.3 %all-to-all-done.4.refs_4_ = bf16[8,512,256]{2,1,0:T(8,128)(2,1)} async-done(((bf16[8,512,256]{2,1,0:T(8,128)(2,1)}), bf16[8,512,256]{2,1,0:T(8,128)(2,1)}, u32[]{:S(2)}, u32[]{:S(2)}) %all-to-all-start.4) | async-done | bytes 2097184 | tf_op jit(solution)/shard_map/all_to_all | solution.py:245
  330.4 4.4 all-to-all-start.5
  334.9 7.2 collective-permute-done.18.refs_1_
  342.1 1.7 collective-permute-start.21
  343.9 2.6 collective-permute-done.20.refs_3_
  346.5 1.4 copy-done.12
  347.9 10.6 %project_and_mix_rows.14 = bf16[8,512,256]{2,1,0:T(8,128)(2,1)} custom-call(s32[1]{0:T(128)} %bitcast.at_ref, bf16[32768,256]{1,0:T(8,128)(2,1)} %refs_0_.15, bf16[4096,256]{1,0:T(8,128)(2,1)} %collective-permute-done.18.refs_1_, bf16[4096,256]{1,0:T(8,128)(2,1)} %copy-done.6, bf16[4096,256]{1,0:T(8,128)(2,1)} %copy-done.12, bf16[1024,256]{1,0:T(8,128)(2,1)} %refs_4_.15, ...), custom_call_target="tpu_custom_call" | custom-call | flops 5368709120 | bytes 10485760 | tf_op jit(solution)/shard_map/project_and_mix_rows/pallas_call | solution.py:95
  358.5 24.0 %all-to-all-done.5.refs_5_ = bf16[8,512,256]{2,1,0:T(8,128)(2,1)} async-done(((bf16[8,512,256]{2,1,0:T(8,128)(2,1)}), bf16[8,512,256]{2,1,0:T(8,128)(2,1)}, u32[]{:S(2)}, u32[]{:S(2)}) %all-to-all-start.5) | async-done | bytes 2097184 | tf_op jit(solution)/shard_map/all_to_all | solution.py:245
  382.5 4.4 all-to-all-start.6
  386.9 3.3 collective-permute-done.21.refs_1_
  391.1 3.6 collective-permute-done.23.refs_3_
  396.0 10.5 %project_and_mix_rows.15 = (bf16[8,512,128]{2,1,0:T(8,128)(2,1)}, bf16[8,512,128]{2,1,0:T(8,128)(2,1)}) custom-call(s32[1]{0:T(128)} %bitcast.at_ref, bf16[32768,256]{1,0:T(8,128)(2,1)} %refs_0_.15, bf16[4096,256]{1,0:T(8,128)(2,1)} %collective-permute-done.21.refs_1_, bf16[4096,256]{1,0:T(8,128)(2,1)} %copy-done.13, bf16[4096,256]{1,0:T(8,128)(2,1)} %copy-done.14, ...), custom_call_target="tpu_custom_call" | custom-call | flops 5368709120 | bytes 10485760 | tf_op jit(solution)/shard_map/project_and_mix_rows/pallas_call | solution.py:95
  406.5 28.1 %all-to-all-done.6.refs_6_ = bf16[8,512,256]{2,1,0:T(8,128)(2,1)} async-done(((bf16[8,512,256]{2,1,0:T(8,128)(2,1)}), bf16[8,512,256]{2,1,0:T(8,128)(2,1)}, u32[]{:S(2)}, u32[]{:S(2)}) %all-to-all-start.6) | async-done | bytes 2097184 | tf_op jit(solution)/shard_map/all_to_all | solution.py:245
  434.7 29.7 %all_to_all.60.refs_7_ = bf16[8,512,128]{2,1,0:T(8,128)(2,1)} all-to-all(bf16[8,512,128]{2,1,0:T(8,128)(2,1)} %get-tuple-element.33), channel_id=1, replica_groups=mesh['tok'=8,'ch'=4] {'tok'}, dimensions={0} | all-to-all | bytes 2097152 | tf_op jit(solution)/shard_map/all_to_all | solution.py:245
  464.4 3.6 all-to-all-start.8
  467.9 28.2 %mix_grid_rows.3 = bf16[8,64,64,128]{3,2,1,0:T(8,128)(2,1)} custom-call(bf16[8,512,256]{2,1,0:T(8,128)(2,1)} %all-to-all-done.refs_0_, bf16[8,512,256]{2,1,0:T(8,128)(2,1)} %all-to-all-done.1.refs_1_, bf16[8,512,256]{2,1,0:T(8,128)(2,1)} %all-to-all-done.2.refs_2_, bf16[8,512,256]{2,1,0:T(8,128)(2,1)} %all-to-all-done.3.refs_3_, ...), custom_call_target="tpu_custom_call" | custom-call | flops 17179869184 | bytes 16777216 | tf_op jit(solution)/shard_map/mix_grid_rows/pallas_call | solution.py:166
  497.2 6.0 all-to-all-start.9
  503.1 28.3 %mix_grid_rows.2 = (bf16[8,56,64,128]{3,2,1,0:T(8,128)(2,1)}, bf16[8,8,64,128]{3,2,1,0:T(8,128)(2,1)}) custom-call(bf16[8,512,256]{2,1,0:T(8,128)(2,1)} %all-to-all-done.refs_0_, bf16[8,512,256]{2,1,0:T(8,128)(2,1)} %all-to-all-done.1.refs_1_, bf16[8,512,256]{2,1,0:T(8,128)(2,1)} %all-to-all-done.2.refs_2_, bf16[8,512,256]{2,1,0:T(8,128)(2,1)} %all-to-all-done.3.refs_3_, ...), custom_call_target="tpu_custom_call" | custom-call | flops 17179869184 | bytes 16777216 | tf_op jit(solution)/shard_map/mix_grid_rows/pallas_call | solution.py:166
  531.4 153.9 %all-to-all-done.9.block_ref = bf16[8,64,64,128]{3,2,1,0:T(8,128)(2,1)} async-done(((bf16[8,64,64,128]{3,2,1,0:T(8,128)(2,1)}), bf16[8,64,64,128]{3,2,1,0:T(8,128)(2,1)}, u32[]{:S(2)}, u32[]{:S(2)}) %all-to-all-start.9) | async-done | bytes 8388640 | tf_op jit(solution)/shard_map/all_to_all | solution.py:245
  685.3 4.9 all-to-all-start.10
  690.1 14.4 %mix_rows_back.3.rest_0_ = bf16[32768,256]{1,0:T(8,128)(2,1)} custom-call(bf16[8,64,64,128]{3,2,1,0:T(8,128)(2,1)} %all-to-all-done.9.block_ref, f32[512,512]{1,0:T(8,128)} %inverse_ref.5), custom_call_target="tpu_custom_call" | custom-call | flops 8589934592 | bytes 16777216 | tf_op jit(solution)/shard_map/mix_rows_back/pallas_call | solution.py:222
  704.6 145.2 %all-to-all-done.10.block_ref = bf16[8,56,64,128]{3,2,1,0:T(8,128)(2,1)} async-done(((bf16[8,56,64,128]{3,2,1,0:T(8,128)(2,1)}), bf16[8,56,64,128]{3,2,1,0:T(8,128)(2,1)}, u32[]{:S(2)}, u32[]{:S(2)}) %all-to-all-start.10) | async-done | bytes 7340064 | tf_op jit(solution)/shard_map/all_to_all | solution.py:245
  849.8 3.7 all-to-all-start.11
  853.4 13.0 %mix_rows_back.4.rest_0_ = bf16[32768,256]{1,0:T(8,128)(2,1)} custom-call(bf16[8,56,64,128]{3,2,1,0:T(8,128)(2,1)} %all-to-all-done.10.block_ref, f32[512,512]{1,0:T(8,128)} %inverse_ref.5, bf16[32768,256]{1,0:T(8,128)(2,1)} %mix_rows_back.3.rest_0_), custom_call_target="tpu_custom_call", output_to_operand_aliasing={{}: (2, {})} | custom-call | flops 7516192768 | bytes 14680064 | tf_op jit(solution)/shard_map/mix_rows_back/pallas_call | solution.py:222
  866.4 13.0 %all-to-all-done.11.block_ref = bf16[8,8,64,128]{3,2,1,0:T(8,128)(2,1)S(1)} async-done(((bf16[8,8,64,128]{3,2,1,0:T(8,128)(2,1)}), bf16[8,8,64,128]{3,2,1,0:T(8,128)(2,1)S(1)}, u32[]{:S(2)}, u32[]{:S(2)}) %all-to-all-start.11) | async-done | bytes 1048608 | tf_op jit(solution)/shard_map/all_to_all | solution.py:245
  880.4 3.9 mix_rows_back.5
  (54 shorter events, 8.8 us)
Async XLA Ops:
  3.0 48.9 %collective-permute-start = (bf16[4096,256]{1,0:T(8,128)(2,1)}, bf16[4096,256]{1,0:T(8,128)(2,1)}, u32[]{:S(2)}, u32[]{:S(2)}) collective-permute-start(bf16[4096,256]{1,0:T(8,128)(2,1)} %slice.24), channel_id=1, source_target_pairs={{0,2},{1,3},{2,0},{3,1},{4,6},{5,7},{6,4},{7,5},{8,10},{9,11},{10,... | collective-permute-start | bytes 6291464 | tf_op jit(solution)/shard_map/ppermute | solution.py:241
  16.2 37.5 %collective-permute-start.1 = (bf16[4096,256]{1,0:T(8,128)(2,1)}, bf16[4096,256]{1,0:T(8,128)(2,1)}, u32[]{:S(2)}, u32[]{:S(2)}) collective-permute-start(bf16[4096,256]{1,0:T(8,128)(2,1)} %slice.24), channel_id=1, source_target_pairs={{0,1},{1,0},{2,3},{3,2},{4,5},{5,4},{6,7},{7,6},{8,9},{9,8},{10,11... | collective-permute-start | bytes 6291464 | tf_op jit(solution)/shard_map/ppermute | solution.py:241
  52.0 4.5 collective-permute-start.2
  52.0 48.4 %collective-permute-start.3 = (bf16[4096,256]{1,0:T(8,128)(2,1)}, bf16[4096,256]{1,0:T(8,128)(2,1)}, u32[]{:S(2)}, u32[]{:S(2)}) collective-permute-start(bf16[4096,256]{1,0:T(8,128)(2,1)} %get-tuple-element.47), channel_id=1, source_target_pairs={{0,2},{1,3},{2,0},{3,1},{4,6},{5,7},{6,4},{7,5},{8,10},{9,11},{10,... | collective-permute-start | bytes 6291464 | tf_op jit(solution)/shard_map/ppermute | solution.py:241
  67.0 54.7 %all-to-all-start = ((bf16[8,512,256]{2,1,0:T(8,128)(2,1)}), bf16[8,512,256]{2,1,0:T(8,128)(2,1)}, u32[]{:S(2)}, u32[]{:S(2)}) async-start(bf16[8,512,256]{2,1,0:T(8,128)(2,1)} %project_and_mix_rows.8), calls=%async_computation | async-start | bytes 4194304 | tf_op jit(solution)/shard_map/all_to_all | solution.py:245
  73.0 29.0 %collective-permute-start.4 = (bf16[4096,256]{1,0:T(8,128)(2,1)}, bf16[4096,256]{1,0:T(8,128)(2,1)S(1)}, u32[]{:S(2)}, u32[]{:S(2)}) collective-permute-start(bf16[4096,256]{1,0:T(8,128)(2,1)} %get-tuple-element.47), channel_id=1, source_target_pairs={{0,1},{1,0},{2,3},{3,2},{4,5},{5,4},{6,7},{7,6},{8,9},{9,8},{10,11... | collective-permute-start | bytes 6291464 | tf_op jit(solution)/shard_map/ppermute | solution.py:241
  100.3 4.4 collective-permute-start.5
  100.3 48.4 %collective-permute-start.6 = (bf16[4096,256]{1,0:T(8,128)(2,1)}, bf16[4096,256]{1,0:T(8,128)(2,1)}, u32[]{:S(2)}, u32[]{:S(2)}) collective-permute-start(bf16[4096,256]{1,0:T(8,128)(2,1)} %get-tuple-element.46), channel_id=1, source_target_pairs={{0,2},{1,3},{2,0},{3,1},{4,6},{5,7},{6,4},{7,5},{8,10},{9,11},{10,... | collective-permute-start | bytes 6291464 | tf_op jit(solution)/shard_map/ppermute | solution.py:241
  102.1 2.6 copy-start.1
  104.7 1.3 copy-start.7
  121.7 52.2 %all-to-all-start.1 = ((bf16[8,512,256]{2,1,0:T(8,128)(2,1)}), bf16[8,512,256]{2,1,0:T(8,128)(2,1)}, u32[]{:S(2)}, u32[]{:S(2)}) async-start(bf16[8,512,256]{2,1,0:T(8,128)(2,1)} %project_and_mix_rows.9), calls=%async_computation.1 | async-start | bytes 4194304 | tf_op jit(solution)/shard_map/all_to_all | solution.py:245
  126.0 24.4 %collective-permute-start.7 = (bf16[4096,256]{1,0:T(8,128)(2,1)}, bf16[4096,256]{1,0:T(8,128)(2,1)S(1)}, u32[]{:S(2)}, u32[]{:S(2)}) collective-permute-start(bf16[4096,256]{1,0:T(8,128)(2,1)} %get-tuple-element.46), channel_id=1, source_target_pairs={{0,1},{1,0},{2,3},{3,2},{4,5},{5,4},{6,7},{7,6},{8,9},{9,8},{10,11... | collective-permute-start | bytes 6291464 | tf_op jit(solution)/shard_map/ppermute | solution.py:241
  148.7 4.4 collective-permute-start.8
  148.7 48.4 %collective-permute-start.9 = (bf16[4096,256]{1,0:T(8,128)(2,1)}, bf16[4096,256]{1,0:T(8,128)(2,1)}, u32[]{:S(2)}, u32[]{:S(2)}) collective-permute-start(bf16[4096,256]{1,0:T(8,128)(2,1)} %get-tuple-element.45), channel_id=1, source_target_pairs={{0,2},{1,3},{2,0},{3,1},{4,6},{5,7},{6,4},{7,5},{8,10},{9,11},{10,... | collective-permute-start | bytes 6291464 | tf_op jit(solution)/shard_map/ppermute | solution.py:241
  150.4 2.6 copy-start.2
  153.1 1.3 copy-start.8
  173.8 52.2 %all-to-all-start.2 = ((bf16[8,512,256]{2,1,0:T(8,128)(2,1)}), bf16[8,512,256]{2,1,0:T(8,128)(2,1)}, u32[]{:S(2)}, u32[]{:S(2)}) async-start(bf16[8,512,256]{2,1,0:T(8,128)(2,1)} %project_and_mix_rows.10), calls=%async_computation.2 | async-start | bytes 4194304 | tf_op jit(solution)/shard_map/all_to_all | solution.py:245
  178.2 20.6 %collective-permute-start.10 = (bf16[4096,256]{1,0:T(8,128)(2,1)}, bf16[4096,256]{1,0:T(8,128)(2,1)S(1)}, u32[]{:S(2)}, u32[]{:S(2)}) collective-permute-start(bf16[4096,256]{1,0:T(8,128)(2,1)} %get-tuple-element.45), channel_id=1, source_target_pairs={{0,1},{1,0},{2,3},{3,2},{4,5},{5,4},{6,7},{7,6},{8,9},{9,8},{10,11... | collective-permute-start | bytes 6291464 | tf_op jit(solution)/shard_map/ppermute | solution.py:241
  197.0 4.4 collective-permute-start.11
  197.0 48.4 %collective-permute-start.12 = (bf16[4096,256]{1,0:T(8,128)(2,1)}, bf16[4096,256]{1,0:T(8,128)(2,1)}, u32[]{:S(2)}, u32[]{:S(2)}) collective-permute-start(bf16[4096,256]{1,0:T(8,128)(2,1)} %get-tuple-element.44), channel_id=1, source_target_pairs={{0,2},{1,3},{2,0},{3,1},{4,6},{5,7},{6,4},{7,5},{8,10},{9,11},{10,... | collective-permute-start | bytes 6291464 | tf_op jit(solution)/shard_map/ppermute | solution.py:241
  198.8 2.6 copy-start.3
  201.4 1.4 copy-start.9
  226.0 52.2 %all-to-all-start.3 = ((bf16[8,512,256]{2,1,0:T(8,128)(2,1)}), bf16[8,512,256]{2,1,0:T(8,128)(2,1)}, u32[]{:S(2)}, u32[]{:S(2)}) async-start(bf16[8,512,256]{2,1,0:T(8,128)(2,1)} %project_and_mix_rows.11), calls=%async_computation.3 | async-start | bytes 4194304 | tf_op jit(solution)/shard_map/all_to_all | solution.py:245
  230.4 16.8 %collective-permute-start.13 = (bf16[4096,256]{1,0:T(8,128)(2,1)}, bf16[4096,256]{1,0:T(8,128)(2,1)S(1)}, u32[]{:S(2)}, u32[]{:S(2)}) collective-permute-start(bf16[4096,256]{1,0:T(8,128)(2,1)} %get-tuple-element.44), channel_id=1, source_target_pairs={{0,1},{1,0},{2,3},{3,2},{4,5},{5,4},{6,7},{7,6},{8,9},{9,8},{10,11... | collective-permute-start | bytes 6291464 | tf_op jit(solution)/shard_map/ppermute | solution.py:241
  245.4 4.4 collective-permute-start.14
  245.4 48.4 %collective-permute-start.15 = (bf16[4096,256]{1,0:T(8,128)(2,1)}, bf16[4096,256]{1,0:T(8,128)(2,1)}, u32[]{:S(2)}, u32[]{:S(2)}) collective-permute-start(bf16[4096,256]{1,0:T(8,128)(2,1)} %get-tuple-element.43), channel_id=1, source_target_pairs={{0,2},{1,3},{2,0},{3,1},{4,6},{5,7},{6,4},{7,5},{8,10},{9,11},{10,... | collective-permute-start | bytes 6291464 | tf_op jit(solution)/shard_map/ppermute | solution.py:241
  247.2 2.6 copy-start.4
  249.8 1.4 copy-start.10
  278.2 52.3 %all-to-all-start.4 = ((bf16[8,512,256]{2,1,0:T(8,128)(2,1)}), bf16[8,512,256]{2,1,0:T(8,128)(2,1)}, u32[]{:S(2)}, u32[]{:S(2)}) async-start(bf16[8,512,256]{2,1,0:T(8,128)(2,1)} %project_and_mix_rows.12), calls=%async_computation.4 | async-start | bytes 4194304 | tf_op jit(solution)/shard_map/all_to_all | solution.py:245
  282.7 12.8 %collective-permute-start.16 = (bf16[4096,256]{1,0:T(8,128)(2,1)}, bf16[4096,256]{1,0:T(8,128)(2,1)S(1)}, u32[]{:S(2)}, u32[]{:S(2)}) collective-permute-start(bf16[4096,256]{1,0:T(8,128)(2,1)} %get-tuple-element.43), channel_id=1, source_target_pairs={{0,1},{1,0},{2,3},{3,2},{4,5},{5,4},{6,7},{7,6},{8,9},{9,8},{10,11... | collective-permute-start | bytes 6291464 | tf_op jit(solution)/shard_map/ppermute | solution.py:241
  293.8 4.4 collective-permute-start.17
  293.8 48.4 %collective-permute-start.18 = (bf16[4096,256]{1,0:T(8,128)(2,1)}, bf16[4096,256]{1,0:T(8,128)(2,1)}, u32[]{:S(2)}, u32[]{:S(2)}) collective-permute-start(bf16[4096,256]{1,0:T(8,128)(2,1)} %get-tuple-element.42), channel_id=1, source_target_pairs={{0,2},{1,3},{2,0},{3,1},{4,6},{5,7},{6,4},{7,5},{8,10},{9,11},{10,... | collective-permute-start | bytes 6291464 | tf_op jit(solution)/shard_map/ppermute | solution.py:241
  295.5 2.6 copy-start.5
  298.1 1.4 copy-start.11
  330.4 52.1 %all-to-all-start.5 = ((bf16[8,512,256]{2,1,0:T(8,128)(2,1)}), bf16[8,512,256]{2,1,0:T(8,128)(2,1)}, u32[]{:S(2)}, u32[]{:S(2)}) async-start(bf16[8,512,256]{2,1,0:T(8,128)(2,1)} %project_and_mix_rows.13), calls=%async_computation.5 | async-start | bytes 4194304 | tf_op jit(solution)/shard_map/all_to_all | solution.py:245
  334.8 9.1 %collective-permute-start.19 = (bf16[4096,256]{1,0:T(8,128)(2,1)}, bf16[4096,256]{1,0:T(8,128)(2,1)S(1)}, u32[]{:S(2)}, u32[]{:S(2)}) collective-permute-start(bf16[4096,256]{1,0:T(8,128)(2,1)} %get-tuple-element.42), channel_id=1, source_target_pairs={{0,1},{1,0},{2,3},{3,2},{4,5},{5,4},{6,7},{7,6},{8,9},{9,8},{10,11... | collective-permute-start | bytes 6291464 | tf_op jit(solution)/shard_map/ppermute | solution.py:241
  342.1 4.4 collective-permute-start.20
  342.1 48.1 %collective-permute-start.21 = (bf16[4096,256]{1,0:T(8,128)(2,1)S(1)}, bf16[4096,256]{1,0:T(8,128)(2,1)}, u32[]{:S(2)}, u32[]{:S(2)}) collective-permute-start(bf16[4096,256]{1,0:T(8,128)(2,1)S(1)} %get-tuple-element.41), channel_id=1, source_target_pairs={{0,2},{1,3},{2,0},{3,1},{4,6},{5,7},{6,4},{7,5},{8,10},{9,11},{10,... | collective-permute-start | bytes 6291464 | tf_op jit(solution)/shard_map/ppermute | solution.py:241
  343.9 2.6 copy-start.6
  346.5 1.4 copy-start.12
  382.5 52.2 %all-to-all-start.6 = ((bf16[8,512,256]{2,1,0:T(8,128)(2,1)}), bf16[8,512,256]{2,1,0:T(8,128)(2,1)}, u32[]{:S(2)}, u32[]{:S(2)}) async-start(bf16[8,512,256]{2,1,0:T(8,128)(2,1)} %project_and_mix_rows.14), calls=%async_computation.6 | async-start | bytes 4194304 | tf_op jit(solution)/shard_map/all_to_all | solution.py:245
  386.9 4.2 collective-permute-start.22
  390.3 4.4 collective-permute-start.23
  391.1 3.6 copy-start.13
  394.6 1.4 copy-start.14
  464.4 31.8 %all-to-all-start.8 = ((bf16[8,512,128]{2,1,0:T(8,128)(2,1)}), bf16[8,512,128]{2,1,0:T(8,128)(2,1)S(1)}, u32[]{:S(2)}, u32[]{:S(2)}) async-start(bf16[8,512,128]{2,1,0:T(8,128)(2,1)} %get-tuple-element.34), calls=%async_computation.8 | async-start | bytes 2097152 | tf_op jit(solution)/shard_map/all_to_all | solution.py:245
  496.2 1.0 copy-start.15
  497.2 188.1 %all-to-all-start.9 = ((bf16[8,64,64,128]{3,2,1,0:T(8,128)(2,1)}), bf16[8,64,64,128]{3,2,1,0:T(8,128)(2,1)}, u32[]{:S(2)}, u32[]{:S(2)}) async-start(bf16[8,64,64,128]{3,2,1,0:T(8,128)(2,1)} %mix_grid_rows.3), calls=%async_computation.9 | async-start | bytes 16777216 | tf_op jit(solution)/shard_map/all_to_all | solution.py:245
  685.3 164.5 %all-to-all-start.10 = ((bf16[8,56,64,128]{3,2,1,0:T(8,128)(2,1)}), bf16[8,56,64,128]{3,2,1,0:T(8,128)(2,1)}, u32[]{:S(2)}, u32[]{:S(2)}) async-start(bf16[8,56,64,128]{3,2,1,0:T(8,128)(2,1)} %get-tuple-element.39), calls=%async_computation.10 | async-start | bytes 14680064 | tf_op jit(solution)/shard_map/all_to_all | solution.py:245
  849.8 29.6 %all-to-all-start.11 = ((bf16[8,8,64,128]{3,2,1,0:T(8,128)(2,1)}), bf16[8,8,64,128]{3,2,1,0:T(8,128)(2,1)S(1)}, u32[]{:S(2)}, u32[]{:S(2)}) async-start(bf16[8,8,64,128]{3,2,1,0:T(8,128)(2,1)} %get-tuple-element.40), calls=%async_computation.11 | async-start | bytes 2097152 | tf_op jit(solution)/shard_map/all_to_all | solution.py:245
  879.4 1.0 copy-start

commit v2 on v1

--- a/solution.py
+++ b/solution.py
@@ -103,7 +103,7 @@
         + [full(w_value), full(w_gate), full(factor), pl.BlockSpec((rows, BLOCK), lambda s: (begin // rows, 0))],
         out_specs=[full(out) for out in outs],
         out_shape=outs,
-        scratch_shapes=[pltpu.VMEM((BLOCK * rows, HALF), jnp.float32)] * 2
+        scratch_shapes=[pltpu.VMEM(((BLOCK + 1) * rows, HALF), jnp.float32)] * 2
         + [pltpu.VMEM((depth, 2 * channels), jnp.bfloat16), pltpu.VMEM((BLOCK, 128), jnp.float32)],
         compiler_params=params(),
         cost_estimate=pl.CostEstimate(
@@ -178,7 +178,7 @@
         out_specs=[pl.BlockSpec((parts, rows, GROUP, HALF), lambda s: (0, 0, s, 0)) for _, rows in splits],
         out_shape=outs,
         scratch_shapes=[pltpu.VMEM((2 * BLOCK, BLOCK), jnp.bfloat16)] * 2
-        + [pltpu.VMEM((BLOCK, GROUP * HALF), jnp.bfloat16), pltpu.VMEM((BLOCK * GROUP, HALF), jnp.float32)],
+        + [pltpu.VMEM((BLOCK, GROUP * HALF), jnp.bfloat16), pltpu.VMEM(((BLOCK + 1) * GROUP, HALF), jnp.float32)],
         compiler_params=params(),
         cost_estimate=pl.CostEstimate(
             flops=8 * BLOCK * BLOCK * indices * HALF,

time: 886 us -> 885 us (level)
  no operation moved by 1% of the time
where the time goes in v2:
time: 885 us; the launch traced here: 884 us
  waiting for transfers between devices  592 us (67%)
  Pallas kernels  172 us (19%)
  starting transfers between devices  66.2 us (7%)
  blocking collectives  29.7 us (3%)
  local copies, waits for them, and re-layouts  24.8 us (3%)
    all_to_all x11, waiting for transfers between devices, exchange(): return lax.all_to_all(block, 'tok', split_axis=0, concat_axis=0, tiled=True)  428 us
    ppermute x24, waiting for transfers between devices, swap(): return lax.ppermute(x, 'ch', [(at, at ^ bit) for at in range(count)])  164 us
    pallas_call x8, Pallas kernels, first_section(): pl.pallas_call(functools.partial(first_body, order, parts, halves), grid=...  84.5 us
    pallas_call x2, Pallas kernels, middle_section(): pl.pallas_call(functools.partial(middle_body, len(blocks), parts, splits)...  55.8 us
    all_to_all x11, starting transfers between devices, exchange(): return lax.all_to_all(block, 'tok', split_axis=0, concat_axis=0, tiled=True)  50.5 us
    pallas_call x3, Pallas kernels, last_section(): pl.pallas_call(last_body, grid=(rows // group,), in_specs=specs, out_spec...  31.3 us
    all_to_all x1, blocking collectives, exchange(): return lax.all_to_all(block, 'tok', split_axis=0, concat_axis=0, tiled=True)  29.7 us
  transfers between devices with their start and end apart: 35, of which 27 were waited for; matrix products, arithmetic and copies ran while one was open for 1% of the time, Pallas kernels for 19%

profile of v2, /device:TPU:0, one launch (start us, length us, event | category | flops | bytes accessed | tf_op | source)
XLA Modules:
  0.0 883.9 jit_solution(13244363568909287912)
XLA Ops:
  0.0 3.0 slice.24
  3.0 3.0 collective-permute-start
  6.0 10.2 %fusion = (bf16[4096,256]{1,0:T(8,128)(2,1)S(1)}, bf16[4096,256]{1,0:T(8,128)(2,1)}, bf16[4096,256]{1,0:T(8,128)(2,1)}, bf16[4096,256]{1,0:T(8,128)(2,1)}, bf16[...) fusion(bf16[32768,256]{1,0:T(8,128)(2,1)} %refs_0_.15), kind=kLoop, calls=%fused_computation | loop fusion | bytes 29360128 | tf_op jit(solution)/shard_map/slice | solution.py:278
  16.3 35.7 %collective-permute-done.refs_1_ = bf16[4096,256]{1,0:T(8,128)(2,1)} collective-permute-done((bf16[4096,256]{1,0:T(8,128)(2,1)}, bf16[4096,256]{1,0:T(8,128)(2,1)}, u32[]{:S(2)}, u32[]{:S(2)}) %collective-permute-start) | collective-permute-done | bytes 2097184 | tf_op jit(solution)/shard_map/ppermute | solution.py:241
  52.0 1.7 collective-permute-start.3
  53.7 2.8 collective-permute-done.2.refs_3_
  56.5 10.5 %project_and_mix_rows.8 = bf16[8,512,256]{2,1,0:T(8,128)(2,1)} custom-call(s32[1]{0:T(128)} %bitcast.at_ref, bf16[32768,256]{1,0:T(8,128)(2,1)} %refs_0_.15, bf16[4096,256]{1,0:T(8,128)(2,1)} %collective-permute-done.refs_1_, bf16[4096,256]{1,0:T(8,128)(2,1)} %collective-permute-done.1.refs_2_, bf16[4096,256]{1,0:T(8,128)(2,1)} %collective-permute-done.2.refs_3_, ...), custom_call_target="tpu_custom_call" | custom-call | flops 5368709120 | bytes 10485760 | tf_op jit(solution)/shard_map/project_and_mix_rows/pallas_call | solution.py:95
  67.0 6.1 all-to-all-start
  73.0 27.3 %collective-permute-done.3.refs_1_ = bf16[4096,256]{1,0:T(8,128)(2,1)} collective-permute-done((bf16[4096,256]{1,0:T(8,128)(2,1)}, bf16[4096,256]{1,0:T(8,128)(2,1)}, u32[]{:S(2)}, u32[]{:S(2)}) %collective-permute-start.3) | collective-permute-done | bytes 2097184 | tf_op jit(solution)/shard_map/ppermute | solution.py:241
  100.3 1.7 collective-permute-start.6
  102.1 2.6 collective-permute-done.5.refs_3_
  106.0 10.6 %project_and_mix_rows.9 = bf16[8,512,256]{2,1,0:T(8,128)(2,1)} custom-call(s32[1]{0:T(128)} %bitcast.at_ref, bf16[32768,256]{1,0:T(8,128)(2,1)} %refs_0_.15, bf16[4096,256]{1,0:T(8,128)(2,1)} %collective-permute-done.3.refs_1_, bf16[4096,256]{1,0:T(8,128)(2,1)} %copy-done.1, bf16[4096,256]{1,0:T(8,128)(2,1)} %copy-done.7, bf16[1024,256]{1,0:T(8,128)(2,1)} %refs_4_.15, ...), custom_call_target="tpu_custom_call" | custom-call | flops 5368709120 | bytes 10485760 | tf_op jit(solution)/shard_map/project_and_mix_rows/pallas_call | solution.py:95
  116.6 5.1 all-to-all-done.refs_0_
  121.7 4.4 all-to-all-start.1
  126.1 22.6 %collective-permute-done.6.refs_1_ = bf16[4096,256]{1,0:T(8,128)(2,1)} collective-permute-done((bf16[4096,256]{1,0:T(8,128)(2,1)}, bf16[4096,256]{1,0:T(8,128)(2,1)}, u32[]{:S(2)}, u32[]{:S(2)}) %collective-permute-start.6) | collective-permute-done | bytes 2097184 | tf_op jit(solution)/shard_map/ppermute | solution.py:241
  148.7 1.7 collective-permute-start.9
  150.4 2.6 collective-permute-done.8.refs_3_
  154.4 10.6 %project_and_mix_rows.10 = bf16[8,512,256]{2,1,0:T(8,128)(2,1)} custom-call(s32[1]{0:T(128)} %bitcast.at_ref, bf16[32768,256]{1,0:T(8,128)(2,1)} %refs_0_.15, bf16[4096,256]{1,0:T(8,128)(2,1)} %collective-permute-done.6.refs_1_, bf16[4096,256]{1,0:T(8,128)(2,1)} %copy-done.2, bf16[4096,256]{1,0:T(8,128)(2,1)} %copy-done.8, bf16[1024,256]{1,0:T(8,128)(2,1)} %refs_4_.15, ...), custom_call_target="tpu_custom_call" | custom-call | flops 5368709120 | bytes 10485760 | tf_op jit(solution)/shard_map/project_and_mix_rows/pallas_call | solution.py:95
  164.9 8.9 %all-to-all-done.1.refs_1_ = bf16[8,512,256]{2,1,0:T(8,128)(2,1)} async-done(((bf16[8,512,256]{2,1,0:T(8,128)(2,1)}), bf16[8,512,256]{2,1,0:T(8,128)(2,1)}, u32[]{:S(2)}, u32[]{:S(2)}) %all-to-all-start.1) | async-done | bytes 2097184 | tf_op jit(solution)/shard_map/all_to_all | solution.py:245
  173.8 4.3 all-to-all-start.2
  178.2 18.8 %collective-permute-done.9.refs_1_ = bf16[4096,256]{1,0:T(8,128)(2,1)} collective-permute-done((bf16[4096,256]{1,0:T(8,128)(2,1)}, bf16[4096,256]{1,0:T(8,128)(2,1)}, u32[]{:S(2)}, u32[]{:S(2)}) %collective-permute-start.9) | collective-permute-done | bytes 2097184 | tf_op jit(solution)/shard_map/ppermute | solution.py:241
  197.0 1.7 collective-permute-start.12
  198.8 2.6 collective-permute-done.11.refs_3_
  201.4 1.4 copy-done.9
  202.8 10.5 %project_and_mix_rows.11 = bf16[8,512,256]{2,1,0:T(8,128)(2,1)} custom-call(s32[1]{0:T(128)} %bitcast.at_ref, bf16[32768,256]{1,0:T(8,128)(2,1)} %refs_0_.15, bf16[4096,256]{1,0:T(8,128)(2,1)} %collective-permute-done.9.refs_1_, bf16[4096,256]{1,0:T(8,128)(2,1)} %copy-done.3, bf16[4096,256]{1,0:T(8,128)(2,1)} %copy-done.9, bf16[1024,256]{1,0:T(8,128)(2,1)} %refs_4_.15, ...), custom_call_target="tpu_custom_call" | custom-call | flops 5368709120 | bytes 10485760 | tf_op jit(solution)/shard_map/project_and_mix_rows/pallas_call | solution.py:95
  213.3 12.7 %all-to-all-done.2.refs_2_ = bf16[8,512,256]{2,1,0:T(8,128)(2,1)} async-done(((bf16[8,512,256]{2,1,0:T(8,128)(2,1)}), bf16[8,512,256]{2,1,0:T(8,128)(2,1)}, u32[]{:S(2)}, u32[]{:S(2)}) %all-to-all-start.2) | async-done | bytes 2097184 | tf_op jit(solution)/shard_map/all_to_all | solution.py:245
  226.0 4.4 all-to-all-start.3
  230.4 15.0 %collective-permute-done.12.refs_1_ = bf16[4096,256]{1,0:T(8,128)(2,1)} collective-permute-done((bf16[4096,256]{1,0:T(8,128)(2,1)}, bf16[4096,256]{1,0:T(8,128)(2,1)}, u32[]{:S(2)}, u32[]{:S(2)}) %collective-permute-start.12) | collective-permute-done | bytes 2097184 | tf_op jit(solution)/shard_map/ppermute | solution.py:241
  245.4 1.7 collective-permute-start.15
  247.2 2.6 collective-permute-done.14.refs_3_
  251.1 10.6 %project_and_mix_rows.12 = bf16[8,512,256]{2,1,0:T(8,128)(2,1)} custom-call(s32[1]{0:T(128)} %bitcast.at_ref, bf16[32768,256]{1,0:T(8,128)(2,1)} %refs_0_.15, bf16[4096,256]{1,0:T(8,128)(2,1)} %collective-permute-done.12.refs_1_, bf16[4096,256]{1,0:T(8,128)(2,1)} %copy-done.4, bf16[4096,256]{1,0:T(8,128)(2,1)} %copy-done.10, bf16[1024,256]{1,0:T(8,128)(2,1)} %refs_4_.15, ...), custom_call_target="tpu_custom_call" | custom-call | flops 5368709120 | bytes 10485760 | tf_op jit(solution)/shard_map/project_and_mix_rows/pallas_call | solution.py:95
  261.8 16.4 %all-to-all-done.3.refs_3_ = bf16[8,512,256]{2,1,0:T(8,128)(2,1)} async-done(((bf16[8,512,256]{2,1,0:T(8,128)(2,1)}), bf16[8,512,256]{2,1,0:T(8,128)(2,1)}, u32[]{:S(2)}, u32[]{:S(2)}) %all-to-all-start.3) | async-done | bytes 2097184 | tf_op jit(solution)/shard_map/all_to_all | solution.py:245
  278.2 4.6 all-to-all-start.4
  282.8 11.0 %collective-permute-done.15.refs_1_ = bf16[4096,256]{1,0:T(8,128)(2,1)} collective-permute-done((bf16[4096,256]{1,0:T(8,128)(2,1)}, bf16[4096,256]{1,0:T(8,128)(2,1)}, u32[]{:S(2)}, u32[]{:S(2)}) %collective-permute-start.15) | collective-permute-done | bytes 2097184 | tf_op jit(solution)/shard_map/ppermute | solution.py:241
  293.8 1.7 collective-permute-start.18
  295.5 2.6 collective-permute-done.17.refs_3_
  298.1 1.4 copy-done.11
  299.5 10.6 %project_and_mix_rows.13 = bf16[8,512,256]{2,1,0:T(8,128)(2,1)} custom-call(s32[1]{0:T(128)} %bitcast.at_ref, bf16[32768,256]{1,0:T(8,128)(2,1)} %refs_0_.15, bf16[4096,256]{1,0:T(8,128)(2,1)} %collective-permute-done.15.refs_1_, bf16[4096,256]{1,0:T(8,128)(2,1)} %copy-done.5, bf16[4096,256]{1,0:T(8,128)(2,1)} %copy-done.11, bf16[1024,256]{1,0:T(8,128)(2,1)} %refs_4_.15, ...), custom_call_target="tpu_custom_call" | custom-call | flops 5368709120 | bytes 10485760 | tf_op jit(solution)/shard_map/project_and_mix_rows/pallas_call | solution.py:95
  310.1 20.3 %all-to-all-done.4.refs_4_ = bf16[8,512,256]{2,1,0:T(8,128)(2,1)} async-done(((bf16[8,512,256]{2,1,0:T(8,128)(2,1)}), bf16[8,512,256]{2,1,0:T(8,128)(2,1)}, u32[]{:S(2)}, u32[]{:S(2)}) %all-to-all-start.4) | async-done | bytes 2097184 | tf_op jit(solution)/shard_map/all_to_all | solution.py:245
  330.4 4.4 all-to-all-start.5
  334.9 7.2 collective-permute-done.18.refs_1_
  342.1 1.7 collective-permute-start.21
  343.9 2.6 collective-permute-done.20.refs_3_
  346.5 1.4 copy-done.12
  347.9 10.6 %project_and_mix_rows.14 = bf16[8,512,256]{2,1,0:T(8,128)(2,1)} custom-call(s32[1]{0:T(128)} %bitcast.at_ref, bf16[32768,256]{1,0:T(8,128)(2,1)} %refs_0_.15, bf16[4096,256]{1,0:T(8,128)(2,1)} %collective-permute-done.18.refs_1_, bf16[4096,256]{1,0:T(8,128)(2,1)} %copy-done.6, bf16[4096,256]{1,0:T(8,128)(2,1)} %copy-done.12, bf16[1024,256]{1,0:T(8,128)(2,1)} %refs_4_.15, ...), custom_call_target="tpu_custom_call" | custom-call | flops 5368709120 | bytes 10485760 | tf_op jit(solution)/shard_map/project_and_mix_rows/pallas_call | solution.py:95
  358.5 24.0 %all-to-all-done.5.refs_5_ = bf16[8,512,256]{2,1,0:T(8,128)(2,1)} async-done(((bf16[8,512,256]{2,1,0:T(8,128)(2,1)}), bf16[8,512,256]{2,1,0:T(8,128)(2,1)}, u32[]{:S(2)}, u32[]{:S(2)}) %all-to-all-start.5) | async-done | bytes 2097184 | tf_op jit(solution)/shard_map/all_to_all | solution.py:245
  382.5 4.4 all-to-all-start.6
  386.9 3.4 collective-permute-done.21.refs_1_
  391.1 3.6 collective-permute-done.23.refs_3_
  396.0 10.5 %project_and_mix_rows.15 = (bf16[8,512,128]{2,1,0:T(8,128)(2,1)}, bf16[8,512,128]{2,1,0:T(8,128)(2,1)}) custom-call(s32[1]{0:T(128)} %bitcast.at_ref, bf16[32768,256]{1,0:T(8,128)(2,1)} %refs_0_.15, bf16[4096,256]{1,0:T(8,128)(2,1)} %collective-permute-done.21.refs_1_, bf16[4096,256]{1,0:T(8,128)(2,1)} %copy-done.13, bf16[4096,256]{1,0:T(8,128)(2,1)} %copy-done.14, ...), custom_call_target="tpu_custom_call" | custom-call | flops 5368709120 | bytes 10485760 | tf_op jit(solution)/shard_map/project_and_mix_rows/pallas_call | solution.py:95
  406.5 28.1 %all-to-all-done.6.refs_6_ = bf16[8,512,256]{2,1,0:T(8,128)(2,1)} async-done(((bf16[8,512,256]{2,1,0:T(8,128)(2,1)}), bf16[8,512,256]{2,1,0:T(8,128)(2,1)}, u32[]{:S(2)}, u32[]{:S(2)}) %all-to-all-start.6) | async-done | bytes 2097184 | tf_op jit(solution)/shard_map/all_to_all | solution.py:245
  434.6 29.7 %all_to_all.60.refs_7_ = bf16[8,512,128]{2,1,0:T(8,128)(2,1)} all-to-all(bf16[8,512,128]{2,1,0:T(8,128)(2,1)} %get-tuple-element.33), channel_id=1, replica_groups=mesh['tok'=8,'ch'=4] {'tok'}, dimensions={0} | all-to-all | bytes 2097152 | tf_op jit(solution)/shard_map/all_to_all | solution.py:245
  464.4 3.6 all-to-all-start.8
  467.9 27.8 %mix_grid_rows.3 = bf16[8,64,64,128]{3,2,1,0:T(8,128)(2,1)} custom-call(bf16[8,512,256]{2,1,0:T(8,128)(2,1)} %all-to-all-done.refs_0_, bf16[8,512,256]{2,1,0:T(8,128)(2,1)} %all-to-all-done.1.refs_1_, bf16[8,512,256]{2,1,0:T(8,128)(2,1)} %all-to-all-done.2.refs_2_, bf16[8,512,256]{2,1,0:T(8,128)(2,1)} %all-to-all-done.3.refs_3_, ...), custom_call_target="tpu_custom_call" | custom-call | flops 17179869184 | bytes 16777216 | tf_op jit(solution)/shard_map/mix_grid_rows/pallas_call | solution.py:166
  496.8 6.0 all-to-all-start.9
  502.7 27.9 %mix_grid_rows.2 = (bf16[8,56,64,128]{3,2,1,0:T(8,128)(2,1)}, bf16[8,8,64,128]{3,2,1,0:T(8,128)(2,1)}) custom-call(bf16[8,512,256]{2,1,0:T(8,128)(2,1)} %all-to-all-done.refs_0_, bf16[8,512,256]{2,1,0:T(8,128)(2,1)} %all-to-all-done.1.refs_1_, bf16[8,512,256]{2,1,0:T(8,128)(2,1)} %all-to-all-done.2.refs_2_, bf16[8,512,256]{2,1,0:T(8,128)(2,1)} %all-to-all-done.3.refs_3_, ...), custom_call_target="tpu_custom_call" | custom-call | flops 17179869184 | bytes 16777216 | tf_op jit(solution)/shard_map/mix_grid_rows/pallas_call | solution.py:166
  530.7 154.2 %all-to-all-done.9.block_ref = bf16[8,64,64,128]{3,2,1,0:T(8,128)(2,1)} async-done(((bf16[8,64,64,128]{3,2,1,0:T(8,128)(2,1)}), bf16[8,64,64,128]{3,2,1,0:T(8,128)(2,1)}, u32[]{:S(2)}, u32[]{:S(2)}) %all-to-all-start.9) | async-done | bytes 8388640 | tf_op jit(solution)/shard_map/all_to_all | solution.py:245
  684.9 4.9 all-to-all-start.10
  689.8 14.4 %mix_rows_back.3.rest_0_ = bf16[32768,256]{1,0:T(8,128)(2,1)} custom-call(bf16[8,64,64,128]{3,2,1,0:T(8,128)(2,1)} %all-to-all-done.9.block_ref, f32[512,512]{1,0:T(8,128)} %inverse_ref.5), custom_call_target="tpu_custom_call" | custom-call | flops 8589934592 | bytes 16777216 | tf_op jit(solution)/shard_map/mix_rows_back/pallas_call | solution.py:222
  704.2 145.2 %all-to-all-done.10.block_ref = bf16[8,56,64,128]{3,2,1,0:T(8,128)(2,1)} async-done(((bf16[8,56,64,128]{3,2,1,0:T(8,128)(2,1)}), bf16[8,56,64,128]{3,2,1,0:T(8,128)(2,1)}, u32[]{:S(2)}, u32[]{:S(2)}) %all-to-all-start.10) | async-done | bytes 7340064 | tf_op jit(solution)/shard_map/all_to_all | solution.py:245
  849.4 3.7 all-to-all-start.11
  853.1 13.0 %mix_rows_back.4.rest_0_ = bf16[32768,256]{1,0:T(8,128)(2,1)} custom-call(bf16[8,56,64,128]{3,2,1,0:T(8,128)(2,1)} %all-to-all-done.10.block_ref, f32[512,512]{1,0:T(8,128)} %inverse_ref.5, bf16[32768,256]{1,0:T(8,128)(2,1)} %mix_rows_back.3.rest_0_), custom_call_target="tpu_custom_call", output_to_operand_aliasing={{}: (2, {})} | custom-call | flops 7516192768 | bytes 14680064 | tf_op jit(solution)/shard_map/mix_rows_back/pallas_call | solution.py:222
  866.0 13.0 %all-to-all-done.11.block_ref = bf16[8,8,64,128]{3,2,1,0:T(8,128)(2,1)S(1)} async-done(((bf16[8,8,64,128]{3,2,1,0:T(8,128)(2,1)}), bf16[8,8,64,128]{3,2,1,0:T(8,128)(2,1)S(1)}, u32[]{:S(2)}, u32[]{:S(2)}) %all-to-all-start.11) | async-done | bytes 1048608 | tf_op jit(solution)/shard_map/all_to_all | solution.py:245
  880.1 3.9 mix_rows_back.5
  (54 shorter events, 8.8 us)
Async XLA Ops:
  3.0 48.9 %collective-permute-start = (bf16[4096,256]{1,0:T(8,128)(2,1)}, bf16[4096,256]{1,0:T(8,128)(2,1)}, u32[]{:S(2)}, u32[]{:S(2)}) collective-permute-start(bf16[4096,256]{1,0:T(8,128)(2,1)} %slice.24), channel_id=1, source_target_pairs={{0,2},{1,3},{2,0},{3,1},{4,6},{5,7},{6,4},{7,5},{8,10},{9,11},{10,... | collective-permute-start | bytes 6291464 | tf_op jit(solution)/shard_map/ppermute | solution.py:241
  16.2 37.5 %collective-permute-start.1 = (bf16[4096,256]{1,0:T(8,128)(2,1)}, bf16[4096,256]{1,0:T(8,128)(2,1)}, u32[]{:S(2)}, u32[]{:S(2)}) collective-permute-start(bf16[4096,256]{1,0:T(8,128)(2,1)} %slice.24), channel_id=1, source_target_pairs={{0,1},{1,0},{2,3},{3,2},{4,5},{5,4},{6,7},{7,6},{8,9},{9,8},{10,11... | collective-permute-start | bytes 6291464 | tf_op jit(solution)/shard_map/ppermute | solution.py:241
  52.0 4.5 collective-permute-start.2
  52.0 48.4 %collective-permute-start.3 = (bf16[4096,256]{1,0:T(8,128)(2,1)}, bf16[4096,256]{1,0:T(8,128)(2,1)}, u32[]{:S(2)}, u32[]{:S(2)}) collective-permute-start(bf16[4096,256]{1,0:T(8,128)(2,1)} %get-tuple-element.47), channel_id=1, source_target_pairs={{0,2},{1,3},{2,0},{3,1},{4,6},{5,7},{6,4},{7,5},{8,10},{9,11},{10,... | collective-permute-start | bytes 6291464 | tf_op jit(solution)/shard_map/ppermute | solution.py:241
  67.0 54.7 %all-to-all-start = ((bf16[8,512,256]{2,1,0:T(8,128)(2,1)}), bf16[8,512,256]{2,1,0:T(8,128)(2,1)}, u32[]{:S(2)}, u32[]{:S(2)}) async-start(bf16[8,512,256]{2,1,0:T(8,128)(2,1)} %project_and_mix_rows.8), calls=%async_computation | async-start | bytes 4194304 | tf_op jit(solution)/shard_map/all_to_all | solution.py:245
  73.0 29.0 %collective-permute-start.4 = (bf16[4096,256]{1,0:T(8,128)(2,1)}, bf16[4096,256]{1,0:T(8,128)(2,1)S(1)}, u32[]{:S(2)}, u32[]{:S(2)}) collective-permute-start(bf16[4096,256]{1,0:T(8,128)(2,1)} %get-tuple-element.47), channel_id=1, source_target_pairs={{0,1},{1,0},{2,3},{3,2},{4,5},{5,4},{6,7},{7,6},{8,9},{9,8},{10,11... | collective-permute-start | bytes 6291464 | tf_op jit(solution)/shard_map/ppermute | solution.py:241
  100.3 4.4 collective-permute-start.5
  100.3 48.4 %collective-permute-start.6 = (bf16[4096,256]{1,0:T(8,128)(2,1)}, bf16[4096,256]{1,0:T(8,128)(2,1)}, u32[]{:S(2)}, u32[]{:S(2)}) collective-permute-start(bf16[4096,256]{1,0:T(8,128)(2,1)} %get-tuple-element.46), channel_id=1, source_target_pairs={{0,2},{1,3},{2,0},{3,1},{4,6},{5,7},{6,4},{7,5},{8,10},{9,11},{10,... | collective-permute-start | bytes 6291464 | tf_op jit(solution)/shard_map/ppermute | solution.py:241
  102.1 2.6 copy-start.1
  104.7 1.3 copy-start.7
  121.7 52.2 %all-to-all-start.1 = ((bf16[8,512,256]{2,1,0:T(8,128)(2,1)}), bf16[8,512,256]{2,1,0:T(8,128)(2,1)}, u32[]{:S(2)}, u32[]{:S(2)}) async-start(bf16[8,512,256]{2,1,0:T(8,128)(2,1)} %project_and_mix_rows.9), calls=%async_computation.1 | async-start | bytes 4194304 | tf_op jit(solution)/shard_map/all_to_all | solution.py:245
  126.0 24.4 %collective-permute-start.7 = (bf16[4096,256]{1,0:T(8,128)(2,1)}, bf16[4096,256]{1,0:T(8,128)(2,1)S(1)}, u32[]{:S(2)}, u32[]{:S(2)}) collective-permute-start(bf16[4096,256]{1,0:T(8,128)(2,1)} %get-tuple-element.46), channel_id=1, source_target_pairs={{0,1},{1,0},{2,3},{3,2},{4,5},{5,4},{6,7},{7,6},{8,9},{9,8},{10,11... | collective-permute-start | bytes 6291464 | tf_op jit(solution)/shard_map/ppermute | solution.py:241
  148.7 4.4 collective-permute-start.8
  148.7 48.4 %collective-permute-start.9 = (bf16[4096,256]{1,0:T(8,128)(2,1)}, bf16[4096,256]{1,0:T(8,128)(2,1)}, u32[]{:S(2)}, u32[]{:S(2)}) collective-permute-start(bf16[4096,256]{1,0:T(8,128)(2,1)} %get-tuple-element.45), channel_id=1, source_target_pairs={{0,2},{1,3},{2,0},{3,1},{4,6},{5,7},{6,4},{7,5},{8,10},{9,11},{10,... | collective-permute-start | bytes 6291464 | tf_op jit(solution)/shard_map/ppermute | solution.py:241
  150.4 2.6 copy-start.2
  153.1 1.3 copy-start.8
  173.8 52.2 %all-to-all-start.2 = ((bf16[8,512,256]{2,1,0:T(8,128)(2,1)}), bf16[8,512,256]{2,1,0:T(8,128)(2,1)}, u32[]{:S(2)}, u32[]{:S(2)}) async-start(bf16[8,512,256]{2,1,0:T(8,128)(2,1)} %project_and_mix_rows.10), calls=%async_computation.2 | async-start | bytes 4194304 | tf_op jit(solution)/shard_map/all_to_all | solution.py:245
  178.2 20.6 %collective-permute-start.10 = (bf16[4096,256]{1,0:T(8,128)(2,1)}, bf16[4096,256]{1,0:T(8,128)(2,1)S(1)}, u32[]{:S(2)}, u32[]{:S(2)}) collective-permute-start(bf16[4096,256]{1,0:T(8,128)(2,1)} %get-tuple-element.45), channel_id=1, source_target_pairs={{0,1},{1,0},{2,3},{3,2},{4,5},{5,4},{6,7},{7,6},{8,9},{9,8},{10,11... | collective-permute-start | bytes 6291464 | tf_op jit(solution)/shard_map/ppermute | solution.py:241
  197.0 4.4 collective-permute-start.11
  197.0 48.4 %collective-permute-start.12 = (bf16[4096,256]{1,0:T(8,128)(2,1)}, bf16[4096,256]{1,0:T(8,128)(2,1)}, u32[]{:S(2)}, u32[]{:S(2)}) collective-permute-start(bf16[4096,256]{1,0:T(8,128)(2,1)} %get-tuple-element.44), channel_id=1, source_target_pairs={{0,2},{1,3},{2,0},{3,1},{4,6},{5,7},{6,4},{7,5},{8,10},{9,11},{10,... | collective-permute-start | bytes 6291464 | tf_op jit(solution)/shard_map/ppermute | solution.py:241
  198.8 2.6 copy-start.3
  201.4 1.4 copy-start.9
  226.0 52.2 %all-to-all-start.3 = ((bf16[8,512,256]{2,1,0:T(8,128)(2,1)}), bf16[8,512,256]{2,1,0:T(8,128)(2,1)}, u32[]{:S(2)}, u32[]{:S(2)}) async-start(bf16[8,512,256]{2,1,0:T(8,128)(2,1)} %project_and_mix_rows.11), calls=%async_computation.3 | async-start | bytes 4194304 | tf_op jit(solution)/shard_map/all_to_all | solution.py:245
  230.4 16.8 %collective-permute-start.13 = (bf16[4096,256]{1,0:T(8,128)(2,1)}, bf16[4096,256]{1,0:T(8,128)(2,1)S(1)}, u32[]{:S(2)}, u32[]{:S(2)}) collective-permute-start(bf16[4096,256]{1,0:T(8,128)(2,1)} %get-tuple-element.44), channel_id=1, source_target_pairs={{0,1},{1,0},{2,3},{3,2},{4,5},{5,4},{6,7},{7,6},{8,9},{9,8},{10,11... | collective-permute-start | bytes 6291464 | tf_op jit(solution)/shard_map/ppermute | solution.py:241
  245.4 4.4 collective-permute-start.14
  245.4 48.4 %collective-permute-start.15 = (bf16[4096,256]{1,0:T(8,128)(2,1)}, bf16[4096,256]{1,0:T(8,128)(2,1)}, u32[]{:S(2)}, u32[]{:S(2)}) collective-permute-start(bf16[4096,256]{1,0:T(8,128)(2,1)} %get-tuple-element.43), channel_id=1, source_target_pairs={{0,2},{1,3},{2,0},{3,1},{4,6},{5,7},{6,4},{7,5},{8,10},{9,11},{10,... | collective-permute-start | bytes 6291464 | tf_op jit(solution)/shard_map/ppermute | solution.py:241
  247.2 2.6 copy-start.4
  249.8 1.4 copy-start.10
  278.2 52.3 %all-to-all-start.4 = ((bf16[8,512,256]{2,1,0:T(8,128)(2,1)}), bf16[8,512,256]{2,1,0:T(8,128)(2,1)}, u32[]{:S(2)}, u32[]{:S(2)}) async-start(bf16[8,512,256]{2,1,0:T(8,128)(2,1)} %project_and_mix_rows.12), calls=%async_computation.4 | async-start | bytes 4194304 | tf_op jit(solution)/shard_map/all_to_all | solution.py:245
  282.7 12.8 %collective-permute-start.16 = (bf16[4096,256]{1,0:T(8,128)(2,1)}, bf16[4096,256]{1,0:T(8,128)(2,1)S(1)}, u32[]{:S(2)}, u32[]{:S(2)}) collective-permute-start(bf16[4096,256]{1,0:T(8,128)(2,1)} %get-tuple-element.43), channel_id=1, source_target_pairs={{0,1},{1,0},{2,3},{3,2},{4,5},{5,4},{6,7},{7,6},{8,9},{9,8},{10,11... | collective-permute-start | bytes 6291464 | tf_op jit(solution)/shard_map/ppermute | solution.py:241
  293.8 4.4 collective-permute-start.17
  293.8 48.4 %collective-permute-start.18 = (bf16[4096,256]{1,0:T(8,128)(2,1)}, bf16[4096,256]{1,0:T(8,128)(2,1)}, u32[]{:S(2)}, u32[]{:S(2)}) collective-permute-start(bf16[4096,256]{1,0:T(8,128)(2,1)} %get-tuple-element.42), channel_id=1, source_target_pairs={{0,2},{1,3},{2,0},{3,1},{4,6},{5,7},{6,4},{7,5},{8,10},{9,11},{10,... | collective-permute-start | bytes 6291464 | tf_op jit(solution)/shard_map/ppermute | solution.py:241
  295.5 2.6 copy-start.5
  298.1 1.4 copy-start.11
  330.4 52.1 %all-to-all-start.5 = ((bf16[8,512,256]{2,1,0:T(8,128)(2,1)}), bf16[8,512,256]{2,1,0:T(8,128)(2,1)}, u32[]{:S(2)}, u32[]{:S(2)}) async-start(bf16[8,512,256]{2,1,0:T(8,128)(2,1)} %project_and_mix_rows.13), calls=%async_computation.5 | async-start | bytes 4194304 | tf_op jit(solution)/shard_map/all_to_all | solution.py:245
  334.8 9.1 %collective-permute-start.19 = (bf16[4096,256]{1,0:T(8,128)(2,1)}, bf16[4096,256]{1,0:T(8,128)(2,1)S(1)}, u32[]{:S(2)}, u32[]{:S(2)}) collective-permute-start(bf16[4096,256]{1,0:T(8,128)(2,1)} %get-tuple-element.42), channel_id=1, source_target_pairs={{0,1},{1,0},{2,3},{3,2},{4,5},{5,4},{6,7},{7,6},{8,9},{9,8},{10,11... | collective-permute-start | bytes 6291464 | tf_op jit(solution)/shard_map/ppermute | solution.py:241
  342.1 4.4 collective-permute-start.20
  342.1 48.1 %collective-permute-start.21 = (bf16[4096,256]{1,0:T(8,128)(2,1)S(1)}, bf16[4096,256]{1,0:T(8,128)(2,1)}, u32[]{:S(2)}, u32[]{:S(2)}) collective-permute-start(bf16[4096,256]{1,0:T(8,128)(2,1)S(1)} %get-tuple-element.41), channel_id=1, source_target_pairs={{0,2},{1,3},{2,0},{3,1},{4,6},{5,7},{6,4},{7,5},{8,10},{9,11},{10,... | collective-permute-start | bytes 6291464 | tf_op jit(solution)/shard_map/ppermute | solution.py:241
  343.9 2.6 copy-start.6
  346.5 1.4 copy-start.12
  382.5 52.2 %all-to-all-start.6 = ((bf16[8,512,256]{2,1,0:T(8,128)(2,1)}), bf16[8,512,256]{2,1,0:T(8,128)(2,1)}, u32[]{:S(2)}, u32[]{:S(2)}) async-start(bf16[8,512,256]{2,1,0:T(8,128)(2,1)} %project_and_mix_rows.14), calls=%async_computation.6 | async-start | bytes 4194304 | tf_op jit(solution)/shard_map/all_to_all | solution.py:245
  386.8 4.2 collective-permute-start.22
  390.3 4.4 collective-permute-start.23
  391.1 3.6 copy-start.13
  394.6 1.4 copy-start.14
  464.4 31.4 %all-to-all-start.8 = ((bf16[8,512,128]{2,1,0:T(8,128)(2,1)}), bf16[8,512,128]{2,1,0:T(8,128)(2,1)S(1)}, u32[]{:S(2)}, u32[]{:S(2)}) async-start(bf16[8,512,128]{2,1,0:T(8,128)(2,1)} %get-tuple-element.34), calls=%async_computation.8 | async-start | bytes 2097152 | tf_op jit(solution)/shard_map/all_to_all | solution.py:245
  495.8 1.0 copy-start.15
  496.8 188.1 %all-to-all-start.9 = ((bf16[8,64,64,128]{3,2,1,0:T(8,128)(2,1)}), bf16[8,64,64,128]{3,2,1,0:T(8,128)(2,1)}, u32[]{:S(2)}, u32[]{:S(2)}) async-start(bf16[8,64,64,128]{3,2,1,0:T(8,128)(2,1)} %mix_grid_rows.3), calls=%async_computation.9 | async-start | bytes 16777216 | tf_op jit(solution)/shard_map/all_to_all | solution.py:245
  684.9 164.5 %all-to-all-start.10 = ((bf16[8,56,64,128]{3,2,1,0:T(8,128)(2,1)}), bf16[8,56,64,128]{3,2,1,0:T(8,128)(2,1)}, u32[]{:S(2)}, u32[]{:S(2)}) async-start(bf16[8,56,64,128]{3,2,1,0:T(8,128)(2,1)} %get-tuple-element.39), calls=%async_computation.10 | async-start | bytes 14680064 | tf_op jit(solution)/shard_map/all_to_all | solution.py:245
  849.4 29.6 %all-to-all-start.11 = ((bf16[8,8,64,128]{3,2,1,0:T(8,128)(2,1)}), bf16[8,8,64,128]{3,2,1,0:T(8,128)(2,1)S(1)}, u32[]{:S(2)}, u32[]{:S(2)}) async-start(bf16[8,8,64,128]{3,2,1,0:T(8,128)(2,1)} %get-tuple-element.40), calls=%async_computation.11 | async-start | bytes 2097152 | tf_op jit(solution)/shard_map/all_to_all | solution.py:245
  879.0 1.0 copy-start
